TPU v7x, 128 devices: a whole 4x4x4 slice. The times are simulated.
128 devices in a mesh: gx: 32 (over x, y, core), gy: 4 (over z).
Axes of the slice: x: 4, y: 4, z: 4, core: 2. Of those that a mesh axis runs over, the one named last changes fastest.
Arguments:
- coarse: bfloat16 [32, 4, 8, 64, 128], P('gx', 'gy'), may hold values from -6 to 6
- lists: int32 [32, 4, 4], P('gx', 'gy'), may hold values from 0 to 1023, as said below
- interp: bfloat16 [1024, 256, 4, 128], P('gx', 'gy'), may hold values from -0.25 to 0.25
- fine_own: bfloat16 [1024, 256, 128], P('gx', 'gy'), may hold values from -6 to 6
- lift: bfloat16 [64, 128], replicated, may hold values from -0.75 to 0.75
- conv_a: bfloat16 [9, 128, 128], replicated, may hold values from -0.1875 to 0.1875
- conv_b: bfloat16 [9, 128, 128], replicated, may hold values from -0.1875 to 0.1875
- cotangent: bfloat16 [1024, 256, 128], P('gx', 'gy'), may hold values from -8 to 8
Outputs:
- output: bfloat16 [1024, 256, 128], P('gx', 'gy')
- grad_conv_a: float32 [9, 128, 128], P(None, None, 'gx')
- grad_conv_b: float32 [9, 128, 128], P(None, None, 'gx')
- grad_coarse: float32 [32, 4, 8, 64, 128], P('gx', 'gy')
Inputs may be any that keep to these rules, and one draw needn't show every extreme that they name: `lists`: each id names a block of the tile's own coarse tile or of a coarse tile adjacent to it along either or both dimensions.
All inputs are finite; a program needn't handle non-finite values.
Results may differ from a plain program's by a relative error of at most 0.0065.
Values may be sent and summed in bfloat16 or wider, within the bound.
A program may use at most 64 MiB of HBM per device.

v0:
```python
import jax
import jax.numpy as jnp
from jax import lax
from jax.sharding import PartitionSpec as P


def with_halo(block, sides, width):
    for axis, dim in sides:
        count = lax.axis_size(axis)
        forward = [(i, i + 1) for i in range(count - 1)]
        backward = [(target, source) for source, target in forward]
        low = lax.ppermute(
            lax.slice_in_dim(block, block.shape[dim] - width, None, axis=dim), axis, forward
        )
        high = lax.ppermute(lax.slice_in_dim(block, 0, width, axis=dim), axis, backward)
        block = jnp.concatenate([low, block, high], axis=dim)
    return block


def offsets():
    return [(di, dj) for di in (-1, 0, 1) for dj in (-1, 0, 1)]


def conv_valid(padded, weights, rows, cols):
    chans = padded.shape[2]
    total = jnp.zeros((rows * cols, weights.shape[2]), jnp.float32)
    for tap, (di, dj) in enumerate(offsets()):
        piece = padded[1 + di : 1 + di + rows, 1 + dj : 1 + dj + cols].reshape(-1, chans)
        total = total + jnp.dot(piece, weights[tap], preferred_element_type=jnp.float32)
    return total.reshape(rows, cols, -1)


def conv_back(padded, weights, rows, cols):
    chans = padded.shape[2]
    total = jnp.zeros((rows * cols, weights.shape[1]), jnp.float32)
    for tap, (di, dj) in enumerate(offsets()):
        piece = padded[1 - di : 1 - di + rows, 1 - dj : 1 - dj + cols].reshape(-1, chans)
        total = total + lax.dot_general(
            piece, weights[tap], (((1,), (1,)), ((), ())), preferred_element_type=jnp.float32
        )
    return total.reshape(rows, cols, -1)


def weight_grad(padded, grad):
    rows, cols, chans = grad.shape
    flat = grad.reshape(-1, chans)
    parts = []
    for tap, (di, dj) in enumerate(offsets()):
        piece = padded[1 + di : 1 + di + rows, 1 + dj : 1 + dj + cols].reshape(-1, padded.shape[2])
        parts.append(
            lax.dot_general(
                piece, flat, (((0,), (0,)), ((), ())), preferred_element_type=jnp.float32
            )
        )
    return jnp.stack(parts)


def extend(field, width):
    return with_halo(field, (("gx", 0), ("gy", 1)), width)


def derivative(pre):
    sig = jax.nn.sigmoid(pre)
    return sig * (1.0 + pre * (1.0 - sig))


def on_device(coarse, lists, interp, fine_own, lift, conv_a, conv_b, cotangent):
    tile_x = lax.axis_index("gx")
    tile_y = lax.axis_index("gy")
    count_x = lax.axis_size("gx")
    count_y = lax.axis_size("gy")
    blocks_dev, chans_in, cells = (coarse.shape[2], coarse.shape[3], coarse.shape[4])
    rows, cols, chans = fine_own.shape
    listed = lists.shape[2]
    beside_all = with_halo(coarse, (("gx", 0), ("gy", 1)), 1)
    stacked = beside_all.reshape(9 * blocks_dev, chans_in * cells)
    ids = lists[0, 0]
    owner = ids // blocks_dev
    step_x = owner // count_y - tile_x + 1
    step_y = owner % count_y - tile_y + 1
    slots = (step_x * 3 + step_y) * blocks_dev + ids % blocks_dev
    picks = slots[:, None] == jnp.arange(9 * blocks_dev, dtype=jnp.int32)[None, :]
    blocks = jnp.dot(picks.astype(jnp.bfloat16), stacked, preferred_element_type=jnp.float32)
    blocks = blocks.astype(jnp.bfloat16).reshape(listed, chans_in, cells)
    weights3 = interp.reshape(rows * cols, listed, cells)
    regrid = lax.dot_general(
        weights3, blocks, (((1, 2), (0, 2)), ((), ())), preferred_element_type=jnp.float32
    ).astype(jnp.bfloat16)
    field = fine_own.reshape(-1, chans).astype(jnp.float32) + jnp.dot(
        regrid, lift, preferred_element_type=jnp.float32
    )
    field = field.astype(jnp.bfloat16).reshape(rows, cols, chans)
    field_ext = extend(field, 1)
    pre = conv_valid(field_ext, conv_a, rows, cols)
    act = jax.nn.silu(pre).astype(jnp.bfloat16)
    act_ext = extend(act, 1)
    output = (field.astype(jnp.float32) + conv_valid(act_ext, conv_b, rows, cols)).astype(
        jnp.bfloat16
    )
    back_act = conv_back(extend(cotangent, 1), conv_b, rows, cols)
    back_pre = (back_act * derivative(pre)).astype(jnp.bfloat16)
    back_ext = extend(back_pre, 1)
    partial_b = weight_grad(act_ext, cotangent)
    partial_a = weight_grad(field_ext, back_pre)
    back_field = (cotangent.astype(jnp.float32) + conv_back(back_ext, conv_a, rows, cols)).astype(
        jnp.bfloat16
    )
    back_regrid = lax.dot_general(
        back_field.reshape(-1, chans),
        lift,
        (((1,), (1,)), ((), ())),
        preferred_element_type=jnp.float32,
    ).astype(jnp.bfloat16)
    back_blocks = lax.dot_general(
        weights3, back_regrid, (((0,), (0,)), ((), ())), preferred_element_type=jnp.float32
    )
    back_blocks = jnp.transpose(back_blocks, (0, 2, 1)).reshape(listed, chans_in * cells)
    spread = lax.dot_general(
        picks.astype(jnp.float32),
        back_blocks,
        (((0,), (0,)), ((), ())),
        precision=lax.Precision.HIGHEST,
        preferred_element_type=jnp.float32,
    )
    spread = spread.reshape(3, 3, blocks_dev, chans_in, cells)
    gathered = with_halo(spread, (("gx", 0), ("gy", 1)), 1)
    grad_coarse = jnp.zeros((blocks_dev, chans_in, cells), jnp.float32)
    for first in (0, 2, 4):
        for second in (0, 2, 4):
            grad_coarse = grad_coarse + gathered[first, second]
    grad_coarse = grad_coarse.reshape(1, 1, blocks_dev, chans_in, cells)
    total_a, total_b = lax.psum((partial_a, partial_b), ("gx", "gy"))
    span = chans // count_x
    grad_conv_a = lax.dynamic_slice_in_dim(total_a, tile_x * span, span, 2)
    grad_conv_b = lax.dynamic_slice_in_dim(total_b, tile_x * span, span, 2)
    return (output, grad_conv_a, grad_conv_b, grad_coarse)


def solution(mesh):
    placed = (
        P("gx", "gy", None, None, None),
        P("gx", "gy", None),
        P("gx", "gy", None, None),
        P("gx", "gy", None),
        P(),
        P(),
        P(),
        P("gx", "gy", None),
    )
    return jax.shard_map(
        on_device,
        mesh=mesh,
        in_specs=placed,
        out_specs=(
            P("gx", "gy", None),
            P(None, None, "gx"),
            P(None, None, "gx"),
            P("gx", "gy", None, None, None),
        ),
        check_vma=False,
    )
```

profile of v0, /device:TPU:0, one launch (start us, length us, event | category | flops | bytes accessed | tf_op | source)
XLA Modules:
  0.0 311.1 jit_solution(112586246036980875)
XLA Ops:
  7.2 2.1 collective-permute-start
  12.6 4.9 %collective-permute-start.12 = (bf16[1,64,128]{2,1,0:T(8,128)(2,1)S(1)}, bf16[1,64,128]{2,1,0:T(8,128)(2,1)S(1)}, u32[]{:S(2)}, u32[]{:S(2)}) collective-permute-start(bf16[1,64,128]{2,1,0:T(8,128)(2,1)S(1)} %get-tuple-element.67), channel_id=1, source_target_pairs={{0,4},{4,8},{8,12},{12,16},{16,20},{20,24},{24,28},{28,32},{32,36}... | collective-permute-start | bytes 49160 | tf_op jit(solution)/shard_map/ppermute | solution.py:12
  18.4 1.8 pad_maximum_fusion.9
  21.5 4.5 %collective-permute-start.15 = (bf16[34,1,128]{2,1,0:T(2,128)(2,1)S(1)}, bf16[34,1,128]{2,1,0:T(2,128)(2,1)S(1)}, u32[]{:S(2)}, u32[]{:S(2)}) collective-permute-start(bf16[34,1,128]{2,1,0:T(2,128)(2,1)S(1)} %get-tuple-element.50), channel_id=1, source_target_pairs={{0,1},{1,2},{2,3},{4,5},{5,6},{6,7},{8,9},{9,10},{10,11},{12,13},{... | collective-permute-start | bytes 26120 | tf_op jit(solution)/shard_map/ppermute | solution.py:12
  27.7 1.6 pad_maximum_fusion.8
  33.4 4.7 %collective-permute-start.2 = (bf16[3,1,8,64,128]{4,3,2,1,0:T(8,128)(2,1)S(1)}, bf16[3,1,8,64,128]{4,3,2,1,0:T(8,128)(2,1)S(1)}, u32[]{:S(2)}, u32[]{:S(2)}) collective-permute-start(bf16[3,1,8,64,128]{4,3,2,1,0:T(8,128)(2,1)S(1)} %constant_dynamic-update-slice_fusion), channel_id=1, source_target_pairs={{0,1},{1,2},{2,3},{4,5},{5,6},{6,7},{8,9},{9,10},{10,11},{12,13},{... | collective-permute-start | bytes 1179656 | tf_op jit(solution)/shard_map/ppermute | solution.py:12
  39.7 6.0 %collective-permute-done.3 = bf16[3,1,8,64,128]{4,3,2,1,0:T(8,128)(2,1)S(1)} collective-permute-done((bf16[3,1,8,64,128]{4,3,2,1,0:T(8,128)(2,1)S(1)}, bf16[3,1,8,64,128]{4,3,2,1,0:T(8,128)(2,1)S(1)}, u32[]{:S(2)}, u32[]{:S(2)}) %collective-permute-start.3) | collective-permute-done | bytes 393248 | tf_op jit(solution)/shard_map/ppermute | solution.py:15
  45.7 1.7 collective-permute-done.2
  48.3 2.0 fusion.5
  50.4 2.2 collective-permute-start.4
  55.3 1.7 collective-permute-done.5
  57.0 4.4 %collective-permute-start.6 = (bf16[34,1,128]{2,1,0:T(2,128)(2,1)S(1)}, bf16[34,1,128]{2,1,0:T(2,128)(2,1)S(1)}, u32[]{:S(2)}, u32[]{:S(2)}) collective-permute-start(bf16[34,1,128]{2,1,0:T(2,128)(2,1)S(1)} %get-tuple-element.57), channel_id=1, source_target_pairs={{0,1},{1,2},{2,3},{4,5},{5,6},{6,7},{8,9},{9,10},{10,11},{12,13},{... | collective-permute-start | bytes 26120 | tf_op jit(solution)/shard_map/ppermute | solution.py:12
  63.1 4.0 %collective-permute-done.7 = bf16[34,1,128]{2,1,0:T(2,128)(2,1)S(1)} collective-permute-done((bf16[34,1,128]{2,1,0:T(2,128)(2,1)S(1)}, bf16[34,1,128]{2,1,0:T(2,128)(2,1)S(1)}, u32[]{:S(2)}, u32[]{:S(2)}) %collective-permute-start.7) | collective-permute-done | bytes 8736 | tf_op jit(solution)/shard_map/ppermute | solution.py:15
  74.4 3.0 collective-permute-start.8
  78.6 4.0 %collective-permute-start.16 = (bf16[1,64,128]{2,1,0:T(8,128)(2,1)S(1)}, bf16[1,64,128]{2,1,0:T(8,128)(2,1)S(1)}, u32[]{:S(2)}, u32[]{:S(2)}) collective-permute-start(bf16[1,64,128]{2,1,0:T(8,128)(2,1)S(1)} %get-tuple-element.61), channel_id=1, source_target_pairs={{0,4},{4,8},{8,12},{12,16},{16,20},{20,24},{24,28},{28,32},{32,36}... | collective-permute-start | bytes 49160 | tf_op jit(solution)/shard_map/ppermute | solution.py:12
  88.3 4.5 %collective-permute-start.19 = (bf16[34,1,128]{2,1,0:T(2,128)(2,1)S(1)}, bf16[34,1,128]{2,1,0:T(2,128)(2,1)S(1)}, u32[]{:S(2)}, u32[]{:S(2)}) collective-permute-start(bf16[34,1,128]{2,1,0:T(2,128)(2,1)S(1)} %get-tuple-element.45), channel_id=1, source_target_pairs={{0,1},{1,2},{2,3},{4,5},{5,6},{6,7},{8,9},{9,10},{10,11},{12,13},{... | collective-permute-start | bytes 26120 | tf_op jit(solution)/shard_map/ppermute | solution.py:12
  92.9 3.7 %collective-permute-start.10 = (bf16[34,1,128]{2,1,0:T(2,128)(2,1)S(1)}, bf16[34,1,128]{2,1,0:T(2,128)(2,1)S(1)}, u32[]{:S(2)}, u32[]{:S(2)}) collective-permute-start(bf16[34,1,128]{2,1,0:T(2,128)(2,1)S(1)} %get-tuple-element.53), channel_id=1, source_target_pairs={{0,1},{1,2},{2,3},{4,5},{5,6},{6,7},{8,9},{9,10},{10,11},{12,13},{... | collective-permute-start | bytes 26120 | tf_op jit(solution)/shard_map/ppermute | solution.py:12
  101.0 2.1 fusion.82
  129.7 4.5 %collective-permute-start.20 = (f32[1,3,8,64,128]{4,3,2,1,0:T(8,128)}, f32[1,3,8,64,128]{4,3,2,1,0:T(8,128)}, u32[]{:S(2)}, u32[]{:S(2)}) collective-permute-start(f32[1,3,8,64,128]{4,3,2,1,0:T(8,128)} %copy.13), channel_id=1, source_target_pairs={{0,4},{4,8},{8,12},{12,16},{16,20},{20,24},{24,28},{28,32},{32,36}... | collective-permute-start | bytes 2359304 | tf_op jit(solution)/shard_map/ppermute | solution.py:12
  142.6 1.8 fusion.168
  145.6 1.7 fusion.167
  147.4 5.5 %collective-permute-start.22 = (f32[5,1,8,64,128]{4,3,2,1,0:T(8,128)}, f32[5,1,8,64,128]{4,3,2,1,0:T(8,128)}, u32[]{:S(2)}, u32[]{:S(2)}) collective-permute-start(f32[5,1,8,64,128]{4,3,2,1,0:T(8,128)} %get-tuple-element.10), channel_id=1, source_target_pairs={{0,1},{1,2},{2,3},{4,5},{5,6},{6,7},{8,9},{9,10},{10,11},{12,13},{... | collective-permute-start | bytes 3932168 | tf_op jit(solution)/shard_map/ppermute | solution.py:12
  156.7 140.8 %all-reduce.3.cloned.1.call-done = (f32[9,128,128]{2,1,0:T(8,128)}, f32[9,128,128]{2,1,0:T(8,128)}) async-done(((f32[9,128,128]{2,1,0:T(8,128)}, f32[9,128,128]{2,1,0:T(8,128)}), (f32[9,128,128]{2,1,0:T(8,128)}, f32[9,128,128]{2,1,0:T(8,128)})) %all-reduce.3.cloned.1.call-update) | async-done | bytes 1179664 | tf_op jit(solution)/shard_map/psum | solution.py:132
  301.8 2.5 slice_add_fusion
  (192 shorter events, 80.4 us)
Async XLA Ops:
  7.2 290.4 %all-reduce.3.cloned.1.call-start = ((), (), s32[]{:S(2)}) async-start(), calls=%async_computation | async-start | bytes 2359296 | tf_op jit(solution)/shard_map/psum | solution.py:132
  7.2 23.0 %collective-permute-start = (bf16[1,1,8,64,128]{4,3,2,1,0:T(8,128)(2,1)}, bf16[1,1,8,64,128]{4,3,2,1,0:T(8,128)(2,1)}, u32[]{:S(2)}, u32[]{:S(2)}) collective-permute-start(bf16[1,1,8,64,128]{4,3,2,1,0:T(8,128)(2,1)} %param.8), channel_id=1, source_target_pairs={{0,4},{4,8},{8,12},{12,16},{16,20},{20,24},{24,28},{28,32},{32,36}... | collective-permute-start | bytes 393224 | tf_op jit(solution)/shard_map/ppermute | solution.py:12
  9.3 21.9 %collective-permute-start.1 = (bf16[1,1,8,64,128]{4,3,2,1,0:T(8,128)(2,1)}, bf16[1,1,8,64,128]{4,3,2,1,0:T(8,128)(2,1)}, u32[]{:S(2)}, u32[]{:S(2)}) collective-permute-start(bf16[1,1,8,64,128]{4,3,2,1,0:T(8,128)(2,1)} %param.8), channel_id=1, source_target_pairs={{4,0},{8,4},{12,8},{16,12},{20,16},{24,20},{28,24},{32,28},{36,32}... | collective-permute-start | bytes 393224 | tf_op jit(solution)/shard_map/ppermute | solution.py:15
  11.3 7.0 %collective-permute-start.13 = (bf16[1,64,128]{2,1,0:T(8,128)(2,1)S(1)}, bf16[1,64,128]{2,1,0:T(8,128)(2,1)S(1)}, u32[]{:S(2)}, u32[]{:S(2)}) collective-permute-start(bf16[1,64,128]{2,1,0:T(8,128)(2,1)S(1)} %get-tuple-element.66), channel_id=1, source_target_pairs={{4,0},{8,4},{12,8},{16,12},{20,16},{24,20},{28,24},{32,28},{36,32}... | collective-permute-start | bytes 49160 | tf_op jit(solution)/shard_map/ppermute | solution.py:15
  12.6 5.8 %collective-permute-start.12 = (bf16[1,64,128]{2,1,0:T(8,128)(2,1)S(1)}, bf16[1,64,128]{2,1,0:T(8,128)(2,1)S(1)}, u32[]{:S(2)}, u32[]{:S(2)}) collective-permute-start(bf16[1,64,128]{2,1,0:T(8,128)(2,1)S(1)} %get-tuple-element.67), channel_id=1, source_target_pairs={{0,4},{4,8},{8,12},{12,16},{16,20},{20,24},{24,28},{28,32},{32,36}... | collective-permute-start | bytes 49160 | tf_op jit(solution)/shard_map/ppermute | solution.py:12
  20.2 7.5 %collective-permute-start.14 = (bf16[34,1,128]{2,1,0:T(2,128)(2,1)S(1)}, bf16[34,1,128]{2,1,0:T(2,128)(2,1)S(1)}, u32[]{:S(2)}, u32[]{:S(2)}) collective-permute-start(bf16[34,1,128]{2,1,0:T(2,128)(2,1)S(1)} %get-tuple-element.49), channel_id=1, source_target_pairs={{1,0},{2,1},{3,2},{5,4},{6,5},{7,6},{9,8},{10,9},{11,10},{13,12},{... | collective-permute-start | bytes 26120 | tf_op jit(solution)/shard_map/ppermute | solution.py:15
  21.5 6.2 %collective-permute-start.15 = (bf16[34,1,128]{2,1,0:T(2,128)(2,1)S(1)}, bf16[34,1,128]{2,1,0:T(2,128)(2,1)S(1)}, u32[]{:S(2)}, u32[]{:S(2)}) collective-permute-start(bf16[34,1,128]{2,1,0:T(2,128)(2,1)S(1)} %get-tuple-element.50), channel_id=1, source_target_pairs={{0,1},{1,2},{2,3},{4,5},{5,6},{6,7},{8,9},{9,10},{10,11},{12,13},{... | collective-permute-start | bytes 26120 | tf_op jit(solution)/shard_map/ppermute | solution.py:12
  32.1 13.6 %collective-permute-start.3 = (bf16[3,1,8,64,128]{4,3,2,1,0:T(8,128)(2,1)S(1)}, bf16[3,1,8,64,128]{4,3,2,1,0:T(8,128)(2,1)S(1)}, u32[]{:S(2)}, u32[]{:S(2)}) collective-permute-start(bf16[3,1,8,64,128]{4,3,2,1,0:T(8,128)(2,1)S(1)} %constant_dynamic-update-slice_fusion), channel_id=1, source_target_pairs={{1,0},{2,1},{3,2},{5,4},{6,5},{7,6},{9,8},{10,9},{11,10},{13,12},{... | collective-permute-start | bytes 1179656 | tf_op jit(solution)/shard_map/ppermute | solution.py:15
  33.4 13.9 %collective-permute-start.2 = (bf16[3,1,8,64,128]{4,3,2,1,0:T(8,128)(2,1)S(1)}, bf16[3,1,8,64,128]{4,3,2,1,0:T(8,128)(2,1)S(1)}, u32[]{:S(2)}, u32[]{:S(2)}) collective-permute-start(bf16[3,1,8,64,128]{4,3,2,1,0:T(8,128)(2,1)S(1)} %constant_dynamic-update-slice_fusion), channel_id=1, source_target_pairs={{0,1},{1,2},{2,3},{4,5},{5,6},{6,7},{8,9},{9,10},{10,11},{12,13},{... | collective-permute-start | bytes 1179656 | tf_op jit(solution)/shard_map/ppermute | solution.py:12
  50.4 4.9 %collective-permute-start.4 = (bf16[1,64,128]{2,1,0:T(8,128)(2,1)S(1)}, bf16[1,64,128]{2,1,0:T(8,128)(2,1)S(1)}, u32[]{:S(2)}, u32[]{:S(2)}) collective-permute-start(bf16[1,64,128]{2,1,0:T(8,128)(2,1)S(1)} %get-tuple-element.74), channel_id=1, source_target_pairs={{0,4},{4,8},{8,12},{12,16},{16,20},{20,24},{24,28},{28,32},{32,36}... | collective-permute-start | bytes 49160 | tf_op jit(solution)/shard_map/ppermute | solution.py:12
  52.6 4.4 %collective-permute-start.5 = (bf16[1,64,128]{2,1,0:T(8,128)(2,1)S(1)}, bf16[1,64,128]{2,1,0:T(8,128)(2,1)S(1)}, u32[]{:S(2)}, u32[]{:S(2)}) collective-permute-start(bf16[1,64,128]{2,1,0:T(8,128)(2,1)S(1)} %get-tuple-element.75), channel_id=1, source_target_pairs={{4,0},{8,4},{12,8},{16,12},{20,16},{24,20},{28,24},{32,28},{36,32}... | collective-permute-start | bytes 49160 | tf_op jit(solution)/shard_map/ppermute | solution.py:15
  57.0 6.1 %collective-permute-start.6 = (bf16[34,1,128]{2,1,0:T(2,128)(2,1)S(1)}, bf16[34,1,128]{2,1,0:T(2,128)(2,1)S(1)}, u32[]{:S(2)}, u32[]{:S(2)}) collective-permute-start(bf16[34,1,128]{2,1,0:T(2,128)(2,1)S(1)} %get-tuple-element.57), channel_id=1, source_target_pairs={{0,1},{1,2},{2,3},{4,5},{5,6},{6,7},{8,9},{9,10},{10,11},{12,13},{... | collective-permute-start | bytes 26120 | tf_op jit(solution)/shard_map/ppermute | solution.py:12
  61.4 5.6 %collective-permute-start.7 = (bf16[34,1,128]{2,1,0:T(2,128)(2,1)S(1)}, bf16[34,1,128]{2,1,0:T(2,128)(2,1)S(1)}, u32[]{:S(2)}, u32[]{:S(2)}) collective-permute-start(bf16[34,1,128]{2,1,0:T(2,128)(2,1)S(1)} %get-tuple-element.58), channel_id=1, source_target_pairs={{1,0},{2,1},{3,2},{5,4},{6,5},{7,6},{9,8},{10,9},{11,10},{13,12},{... | collective-permute-start | bytes 26120 | tf_op jit(solution)/shard_map/ppermute | solution.py:15
  74.4 18.5 %collective-permute-start.8 = (bf16[1,64,128]{2,1,0:T(8,128)(2,1)S(1)}, bf16[1,64,128]{2,1,0:T(8,128)(2,1)S(1)}, u32[]{:S(2)}, u32[]{:S(2)}) collective-permute-start(bf16[1,64,128]{2,1,0:T(8,128)(2,1)S(1)} %get-tuple-element.70), channel_id=1, source_target_pairs={{0,4},{4,8},{8,12},{12,16},{16,20},{20,24},{24,28},{28,32},{32,36}... | collective-permute-start | bytes 49160 | tf_op jit(solution)/shard_map/ppermute | solution.py:12
  77.3 15.6 %collective-permute-start.9 = (bf16[1,64,128]{2,1,0:T(8,128)(2,1)S(1)}, bf16[1,64,128]{2,1,0:T(8,128)(2,1)S(1)}, u32[]{:S(2)}, u32[]{:S(2)}) collective-permute-start(bf16[1,64,128]{2,1,0:T(8,128)(2,1)S(1)} %get-tuple-element.71), channel_id=1, source_target_pairs={{4,0},{8,4},{12,8},{16,12},{20,16},{24,20},{28,24},{32,28},{36,32}... | collective-permute-start | bytes 49160 | tf_op jit(solution)/shard_map/ppermute | solution.py:15
  78.6 8.3 %collective-permute-start.16 = (bf16[1,64,128]{2,1,0:T(8,128)(2,1)S(1)}, bf16[1,64,128]{2,1,0:T(8,128)(2,1)S(1)}, u32[]{:S(2)}, u32[]{:S(2)}) collective-permute-start(bf16[1,64,128]{2,1,0:T(8,128)(2,1)S(1)} %get-tuple-element.61), channel_id=1, source_target_pairs={{0,4},{4,8},{8,12},{12,16},{16,20},{20,24},{24,28},{28,32},{32,36}... | collective-permute-start | bytes 49160 | tf_op jit(solution)/shard_map/ppermute | solution.py:12
  87.0 18.6 %collective-permute-start.18 = (bf16[34,1,128]{2,1,0:T(2,128)(2,1)S(1)}, bf16[34,1,128]{2,1,0:T(2,128)(2,1)S(1)}, u32[]{:S(2)}, u32[]{:S(2)}) collective-permute-start(bf16[34,1,128]{2,1,0:T(2,128)(2,1)S(1)} %get-tuple-element.44), channel_id=1, source_target_pairs={{1,0},{2,1},{3,2},{5,4},{6,5},{7,6},{9,8},{10,9},{11,10},{13,12},{... | collective-permute-start | bytes 26120 | tf_op jit(solution)/shard_map/ppermute | solution.py:15
  88.3 17.3 %collective-permute-start.19 = (bf16[34,1,128]{2,1,0:T(2,128)(2,1)S(1)}, bf16[34,1,128]{2,1,0:T(2,128)(2,1)S(1)}, u32[]{:S(2)}, u32[]{:S(2)}) collective-permute-start(bf16[34,1,128]{2,1,0:T(2,128)(2,1)S(1)} %get-tuple-element.45), channel_id=1, source_target_pairs={{0,1},{1,2},{2,3},{4,5},{5,6},{6,7},{8,9},{9,10},{10,11},{12,13},{... | collective-permute-start | bytes 26120 | tf_op jit(solution)/shard_map/ppermute | solution.py:12
  92.9 10.1 %collective-permute-start.10 = (bf16[34,1,128]{2,1,0:T(2,128)(2,1)S(1)}, bf16[34,1,128]{2,1,0:T(2,128)(2,1)S(1)}, u32[]{:S(2)}, u32[]{:S(2)}) collective-permute-start(bf16[34,1,128]{2,1,0:T(2,128)(2,1)S(1)} %get-tuple-element.53), channel_id=1, source_target_pairs={{0,1},{1,2},{2,3},{4,5},{5,6},{6,7},{8,9},{9,10},{10,11},{12,13},{... | collective-permute-start | bytes 26120 | tf_op jit(solution)/shard_map/ppermute | solution.py:12
  96.6 6.4 %collective-permute-start.11 = (bf16[34,1,128]{2,1,0:T(2,128)(2,1)S(1)}, bf16[34,1,128]{2,1,0:T(2,128)(2,1)S(1)}, u32[]{:S(2)}, u32[]{:S(2)}) collective-permute-start(bf16[34,1,128]{2,1,0:T(2,128)(2,1)S(1)} %get-tuple-element.54), channel_id=1, source_target_pairs={{1,0},{2,1},{3,2},{5,4},{6,5},{7,6},{9,8},{10,9},{11,10},{13,12},{... | collective-permute-start | bytes 26120 | tf_op jit(solution)/shard_map/ppermute | solution.py:15
  129.7 11.2 %collective-permute-start.20 = (f32[1,3,8,64,128]{4,3,2,1,0:T(8,128)}, f32[1,3,8,64,128]{4,3,2,1,0:T(8,128)}, u32[]{:S(2)}, u32[]{:S(2)}) collective-permute-start(f32[1,3,8,64,128]{4,3,2,1,0:T(8,128)} %copy.13), channel_id=1, source_target_pairs={{0,4},{4,8},{8,12},{12,16},{16,20},{20,24},{24,28},{28,32},{32,36}... | collective-permute-start | bytes 2359304 | tf_op jit(solution)/shard_map/ppermute | solution.py:12
  134.3 10.2 %collective-permute-start.21 = (f32[1,3,8,64,128]{4,3,2,1,0:T(8,128)}, f32[1,3,8,64,128]{4,3,2,1,0:T(8,128)}, u32[]{:S(2)}, u32[]{:S(2)}) collective-permute-start(f32[1,3,8,64,128]{4,3,2,1,0:T(8,128)} %copy.14), channel_id=1, source_target_pairs={{4,0},{8,4},{12,8},{16,12},{20,16},{24,20},{28,24},{32,28},{36,32}... | collective-permute-start | bytes 2359304 | tf_op jit(solution)/shard_map/ppermute | solution.py:15
  147.4 154.4 %collective-permute-start.22 = (f32[5,1,8,64,128]{4,3,2,1,0:T(8,128)}, f32[5,1,8,64,128]{4,3,2,1,0:T(8,128)}, u32[]{:S(2)}, u32[]{:S(2)}) collective-permute-start(f32[5,1,8,64,128]{4,3,2,1,0:T(8,128)} %get-tuple-element.10), channel_id=1, source_target_pairs={{0,1},{1,2},{2,3},{4,5},{5,6},{6,7},{8,9},{9,10},{10,11},{12,13},{... | collective-permute-start | bytes 3932168 | tf_op jit(solution)/shard_map/ppermute | solution.py:12
  152.9 148.9 %collective-permute-start.23 = (f32[5,1,8,64,128]{4,3,2,1,0:T(8,128)}, f32[5,1,8,64,128]{4,3,2,1,0:T(8,128)}, u32[]{:S(2)}, u32[]{:S(2)}) collective-permute-start(f32[5,1,8,64,128]{4,3,2,1,0:T(8,128)} %get-tuple-element.11), channel_id=1, source_target_pairs={{1,0},{2,1},{3,2},{5,4},{6,5},{7,6},{9,8},{10,9},{11,10},{13,12},{... | collective-permute-start | bytes 3932168 | tf_op jit(solution)/shard_map/ppermute | solution.py:15
  (33 other events, 168.8 us)
Sparse Core Ops, SparseCore 0:
  135.9 161.6 all-reduce.2
where the time goes:
time: 313 us; the launch traced here: 311 us
  waiting for transfers between devices  154 us (49%)
  starting transfers between devices  64 us (20%)
  matrix products  35.1 us (11%)
  local copies, waits for them, and re-layouts  31.5 us (10%)
  between operations  15 us (5%)
  other arithmetic  11.3 us (4%)
    psum x1, waiting for transfers between devices, on_device(): total_a, total_b = lax.psum((partial_a, partial_b), ('gx', 'gy'))  141 us
    ppermute x12, starting transfers between devices, with_halo(): lax.ppermute(lax.slice_in_dim(block, block.shape[dim] - width, None, axis...  48.1 us
    ppermute x12, starting transfers between devices, with_halo(): lax.ppermute(lax.slice_in_dim(block, 0, width, axis=dim), axis, backward)  15.9 us
    unnamed x70, local copies, waits for them, and re-layouts  15 us
    dot_general x18, matrix products, weight_grad(): lax.dot_general(piece, flat, (((0,), (0,)), ((), ())), preferred_element_...  11.8 us
    ppermute x12, waiting for transfers between devices, with_halo(): lax.ppermute(lax.slice_in_dim(block, 0, width, axis=dim), axis, backward)  11.7 us
    dot_general x18, matrix products, conv_back(): lax.dot_general(piece, weights[tap], (((1,), (1,)), ((), ())), preferred_...  10.4 us
    dot_general x18, matrix products, conv_valid(): jnp.dot(piece, weights[tap], preferred_element_type=jnp.float32)  8.21 us
  transfers between devices with their start and end apart: 25, of which 6 were waited for; matrix products, arithmetic and copies ran while one was open for 12% of the time, Pallas kernels for 0%

commit v1 on v0

v1 whole, which is shorter than its diff:
```python
import functools

import jax
import jax.numpy as jnp
from jax import lax
from jax.experimental import pallas as pl
from jax.experimental.pallas import tpu as pltpu
from jax.sharding import PartitionSpec as P

MESH = pl.DeviceIdType.MESH
F32 = jnp.float32
BF16 = jnp.bfloat16
MIB = 1024 * 1024
NT = (((1,), (1,)), ((), ()))


class Sizes:
    def __init__(self, gx, gy, nx, ny, rows, cols, chans, chans_in, cells, listed, blocks):
        self.gx, self.gy, self.nx, self.ny = gx, gy, nx, ny
        self.rows, self.cols = rows, cols
        self.chans, self.chans_in, self.cells = chans, chans_in, cells
        self.listed, self.blocks = listed, blocks
        self.px = rows * cols
        self.width = cols + 32
        self.ext = cols + 16
        self.span = chans // gx
        self.pack = -(-3 * self.span // 16) * 16
        self.taps = 9 * chans
        self.ch_main = 4 if rows % 4 == 0 else rows
        self.ch_ext = 2


def kernel(
    sz,
    lists, coarse, interp, fine, lift, wa, wb, cot,
    out, ga, gb, gc,
    call, lvec, lrecv, lsm, picked, crecv,
    raw, rawf, interp2, fine_v, lift_v, wa_v, wb_v, wat, wbt, cot_v, bt,
    x_cot, x_field, x_act, x_bp, a_cot, a_field, a_act, a_bp,
    back_act, field, out_v, cot_t, bp_t,
    hs_cols, hs_corner, hr_rows, hr_cols, hr_corner,
    wsum, wsend, w1, wst2, w2, w3,
    gsum, gsend, g1, g2send, g2, gacc,
    local_sem, lsem, csend, crcv, hsend, hrcv, wsnd, wrcv, gsnd, grcv,
):
    tx = lax.axis_index("gx")
    ty = lax.axis_index("gy")
    gx, gy, nx, ny = sz.gx, sz.gy, sz.nx, sz.ny
    rows, cols, chans, width, ext, px = sz.rows, sz.cols, sz.chans, sz.width, sz.ext, sz.px
    core = tx % 2
    cy = (tx // 2) % ny
    cx = tx // (2 * ny)
    left, right = (tx + gx - 1) % gx, (tx + 1) % gx
    down, up = (ty + gy - 1) % gy, (ty + 1) % gy
    started = []

    def remote(src, dst, ssem, rsem, px_, py_):
        copy = pltpu.make_async_remote_copy(
            src_ref=src, dst_ref=dst, send_sem=ssem, recv_sem=rsem,
            device_id=(px_, py_), device_id_type=MESH,
        )
        copy.start()
        started.append(copy)
        return copy

    def local(src, dst, i):
        copy = pltpu.make_async_copy(src, dst, local_sem.at[i])
        copy.start()
        return copy

    ld_coarse = local(coarse, call.at[1], 0)
    ld_cot = local(cot, cot_v, 1)
    ld_raw = local(interp, raw, 2)
    ld_wb = local(wb, wb_v, 3)
    ld_wa = local(wa, wa_v, 4)
    ld_fine = local(fine, fine_v, 5)
    ld_lift = local(lift, lift_v, 6)

    halo = [(left, ty), (right, ty), (tx, down), (tx, up),
            (left, down), (left, up), (right, down), (right, up)]
    peers = list(halo)
    for o in range(2, gy - 1):
        peers.append((tx, (ty + o) % gy))
    for o in range(1, ny):
        for c in range(2):
            peers.append((((cx * ny + (cy + o) % ny) * 2 + c), ty))
    for o in range(1, nx):
        for c in range(2):
            peers.append(((((cx + o) % nx) * ny + cy) * 2 + c, ty))
    barrier = pltpu.get_barrier_semaphore()
    for p in peers:
        pl.semaphore_signal(barrier, inc=1, device_id=p, device_id_type=MESH)
    rowi = lax.broadcasted_iota(jnp.int32, (8, 128), 0)
    vec = jnp.zeros((8, 128), jnp.int32)
    for k in range(sz.listed):
        vec = jnp.where(rowi == k, lists[0, k], vec)
    lvec[...] = vec
    ld_coarse.wait()
    pl.semaphore_wait(barrier, len(peers))

    c1 = [remote(call.at[1], call.at[2], csend.at[0], crcv.at[0], left, ty),
          remote(call.at[1], call.at[0], csend.at[1], crcv.at[1], right, ty)]
    l1 = [remote(lvec, lrecv.at[1], csend.at[2], crcv.at[2], tx, down),
          remote(lvec, lrecv.at[0], csend.at[3], crcv.at[3], tx, up)]

    def fill(x, src):
        def body(r, _):
            x[pl.ds(pl.multiple_of((r + 2) * width + 16, 16), cols), :] = src[
                pl.ds(pl.multiple_of(r * cols, cols), cols), :].astype(F32)
            return 0
        lax.fori_loop(0, rows, body, 0)

    def rim_send(e, x, main):
        cps = []
        n2 = 2 * cols
        cps.append(remote(main.at[pl.ds(0, n2), :], hr_rows.at[e, 1],
                          hsend.at[e, 0], hrcv.at[e, 0], left, ty))
        cps.append(remote(main.at[pl.ds(px - n2, n2), :], hr_rows.at[e, 0],
                          hsend.at[e, 1], hrcv.at[e, 1], right, ty))
        for s, c0 in ((0, 0), (1, cols - 2)):
            for j in range(2):
                hs_cols[e, s, j * rows:(j + 1) * rows, :] = x[
                    pl.ds(2 * width + 16 + c0 + j, rows, stride=width), :].astype(BF16)
        cps.append(remote(hs_cols.at[e, 0], hr_cols.at[e, 1],
                          hsend.at[e, 2], hrcv.at[e, 2], tx, down))
        cps.append(remote(hs_cols.at[e, 1], hr_cols.at[e, 0],
                          hsend.at[e, 3], hrcv.at[e, 3], tx, up))
        q = 0
        for sr, r0, tox in ((0, 0, left), (1, rows - 2, right)):
            for sc, c0, toy in ((0, 0, down), (1, cols - 2, up)):
                parts = [x[(2 + r0 + i) * width + 16 + c0:(2 + r0 + i) * width + 18 + c0, :]
                         for i in range(2)]
                parts.append(jnp.zeros((12, chans), F32))
                hs_corner[e, q] = jnp.concatenate(parts, axis=0).astype(BF16)
                cps.append(remote(hs_corner.at[e, q], hr_corner.at[e, 3 - q],
                                  hsend.at[e, 4 + q], hrcv.at[e, 4 + q], tox, toy))
                q += 1
        return cps

    in_x = (tx > 0, tx < gx - 1)
    in_y = (ty > 0, ty < gy - 1)

    def rim_take(e, x, cps):
        for cp in cps:
            cp.wait_recv()
        for s, r0 in ((0, 0), (1, rows + 2)):
            v = jnp.where(in_x[s], hr_rows[e, s].astype(F32), 0.0)
            for i in range(2):
                x[(r0 + i) * width + 16:(r0 + i) * width + 16 + cols, :] = v[i * cols:(i + 1) * cols]
        for s, c0 in ((0, 14), (1, 16 + cols)):
            v = jnp.where(in_y[s], hr_cols[e, s].astype(F32), 0.0)
            for j in range(2):
                x[pl.ds(2 * width + c0 + j, rows, stride=width), :] = v[j * rows:(j + 1) * rows]
        q = 0
        for sr, r0 in ((0, 0), (1, rows + 2)):
            for sc, c0 in ((0, 14), (1, 16 + cols)):
                v = jnp.where(jnp.logical_and(in_x[sr], in_y[sc]),
                              hr_corner[e, q].astype(F32), 0.0)
                for i in range(2):
                    x[(r0 + i) * width + c0:(r0 + i) * width + c0 + 2, :] = v[2 * i:2 * i + 2]
                q += 1

    def widen(x, a):
        def body(r, _):
            base = pl.multiple_of(r * width, 16)
            for dj in range(3):
                v = x[pl.ds(base + 15 + dj, cols + 8), :]
                w = x[pl.ds(base + 7 + dj, 8), :]
                a[r, :, dj * chans:(dj + 1) * chans] = jnp.concatenate([v, w], axis=0).astype(BF16)
            return 0
        lax.fori_loop(0, rows + 4, body, 0)

    def widen_main(x, a):
        def body(r, _):
            base = pl.multiple_of((r + 1) * width, 16)
            for dj in range(3):
                a[pl.ds(pl.multiple_of(r * cols, cols), cols), dj * chans:(dj + 1) * chans] = x[
                    pl.ds(base + 15 + dj, cols), :].astype(BF16)
            return 0
        lax.fori_loop(0, rows + 2, body, 0)

    def conv_ext(a, w, r, n):
        v = jnp.concatenate(
            [a[pl.ds(r + d, n)].reshape(n * ext, 3 * chans) for d in range(3)], axis=1)
        return jnp.dot(v, w[...], preferred_element_type=F32)

    def conv_main(a, w, r, n):
        v = jnp.concatenate(
            [a[pl.ds(pl.multiple_of((r + d) * cols, cols), n * cols), :] for d in range(3)], axis=1)
        return jnp.dot(v, w[...], preferred_element_type=F32)

    ld_cot.wait()
    fill(x_cot, cot_v)
    h_cot = rim_send(0, x_cot, cot_v)

    ld_wb.wait()
    ld_wa.wait()
    for src, dst in ((wb_v, wbt), (wa_v, wat)):
        for t in range(9):
            dst[t * chans:(t + 1) * chans, :] = src[
                (8 - t) * chans:(9 - t) * chans, :].astype(F32).T.astype(BF16)

    ld_raw.wait()
    step = px // 8
    listed, cells, chans_in = sz.listed, sz.cells, sz.chans_in

    def relay(i, _):
        rawf[...] = raw[pl.ds(pl.multiple_of(i * step * listed, 16), step * listed), :].astype(F32)
        for k in range(listed):
            interp2[pl.ds(pl.multiple_of(i * step, 16), step), k * cells:(k + 1) * cells] = rawf[
                pl.ds(k, step, stride=listed), :].astype(BF16)
        return 0
    lax.fori_loop(0, 8, relay, 0)

    for cp in c1 + l1:
        cp.wait_recv()
    ld_l = pltpu.make_async_copy(lrecv, lsm, lsem)
    ld_l.start()
    ld_l.wait()

    def clip(v):
        return jnp.minimum(jnp.maximum(v, 0), 2)

    nb = sz.blocks
    c2 = []
    for s, toy in ((0, down), (1, up)):
        for k in range(listed):
            i = lsm[s, k, 0]
            picked[s, k] = call[clip(i // (nb * gy) - tx + 1), i % nb]
        c2.append(remote(picked.at[s], crecv.at[1 - s], csend.at[4 + s], crcv.at[4 + s], tx, toy))
    ids = [lists[0, k] for k in range(listed)]
    for k in range(listed):
        i = ids[k]
        crecv[2, k] = call[clip(i // (nb * gy) - tx + 1), i % nb]

    rim_take(0, x_cot, h_cot)
    widen(x_cot, a_cot)
    ce = sz.ch_ext

    def back_body(i, _):
        back_act[pl.ds(pl.multiple_of(i * (ce * ext), 16), ce * ext), :] = conv_ext(
            a_cot, wbt, i * ce, ce)
        return 0
    lax.fori_loop(0, (rows + 2) // ce, back_body, 0)

    ri = lax.broadcasted_iota(jnp.int32, (chans, chans), 0)
    ci = lax.broadcasted_iota(jnp.int32, (chans, chans), 1)
    span = sz.span

    def order(first, second, first_is_y):
        m, rest = ri // (second * span), ri % (second * span)
        s, j = rest // span, rest % span
        if first_is_y:
            return (s * ny + m // 2) * 2 * span + (m % 2) * span + j
        return ((m // 2) * ny + s) * 2 * span + (m % 2) * span + j

    perm_b = jnp.where(ci == order(ny, nx, True), 1.0, 0.0).astype(BF16)
    perm_a = jnp.where(ci == order(nx, ny, False), 1.0, 0.0).astype(BF16)
    cm = sz.ch_main
    pc = cm * cols

    def turn_cot(i, _):
        q = pl.multiple_of(i * pc, 128)
        cot_t[:, pl.ds(q, pc)] = lax.dot_general(
            perm_b, cot_v[pl.ds(q, pc), :], NT, preferred_element_type=F32).astype(BF16)
        return 0
    lax.fori_loop(0, px // pc, turn_cot, 0)

    for cp in c2:
        cp.wait_recv()
    for k in range(listed):
        oy = (ids[k] // nb) % gy
        which = jnp.where(oy == ty, 2, jnp.where(oy < ty, 0, 1))
        bt[k * cells:(k + 1) * cells, :] = crecv[which, k].astype(F32).T.astype(BF16)
    ld_fine.wait()
    ld_lift.wait()

    def regrid_body(i, _):
        q = pl.multiple_of(i * pc, 128)
        g = jnp.dot(interp2[pl.ds(q, pc), :], bt[...], preferred_element_type=F32).astype(BF16)
        f = fine_v[pl.ds(q, pc), :].astype(F32) + jnp.dot(
            g, lift_v[...], preferred_element_type=F32)
        f = f.astype(BF16)
        field[pl.ds(q, pc), :] = f
        f = f.astype(F32)
        for r in range(cm):
            x_field[pl.ds(pl.multiple_of((i * cm + r + 2) * width + 16, 16), cols), :] = f[
                r * cols:(r + 1) * cols]
        return 0
    lax.fori_loop(0, px // pc, regrid_body, 0)

    h_field = rim_send(1, x_field, field)
    rim_take(1, x_field, h_field)
    widen(x_field, a_field)

    def pre_body(i, _):
        pre = conv_ext(a_field, wa_v, i * ce, ce)
        sig = 1.0 / (1.0 + jnp.exp(-pre))
        act = pre * sig
        bp = back_act[pl.ds(pl.multiple_of(i * (ce * ext), 16), ce * ext), :] * (
            sig * (1.0 + pre * (1.0 - sig)))
        for x, v in ((x_act, act), (x_bp, bp)):
            for r in range(ce):
                base = pl.multiple_of((i * ce + r + 1) * width, 16)
                o = r * ext
                x[pl.ds(base + 16, cols), :] = v[o:o + cols]
                x[pl.ds(base + 16 + cols, 8), :] = jnp.where(in_y[1], v[o + cols:o + cols + 8], 0.0)
                x[pl.ds(base + 8, 8), :] = jnp.where(in_y[0], v[o + cols + 8:o + ext], 0.0)
        return 0
    lax.fori_loop(0, (rows + 2) // ce, pre_body, 0)

    for inside, r in ((in_x[0], 1), (in_x[1], rows + 2)):
        @pl.when(jnp.logical_not(inside))
        def _():
            for x in (x_act, x_bp):
                x[r * width:(r + 1) * width, :] = jnp.zeros((width, chans), F32)

    widen_main(x_act, a_act)
    widen_main(x_bp, a_bp)

    def weight_grad(w, lhs, get):
        v = jnp.concatenate([get(d) for d in range(3)], axis=1)
        g = jnp.dot(lhs[...], v, preferred_element_type=F32)
        wsum[w] = g
        wsend[w] = g.astype(BF16)

    npx = px

    def first(w):
        n = 2 * (ny if w else nx)
        chunk = chans // n
        m = (cy if w else cx) * 2 + core
        cps = []
        for o in range(1, n):
            t = (m + o) % n
            peer = ((cx * ny + t // 2) if w else ((t // 2) * ny + cy)) * 2 + t % 2
            cps.append(remote(wsend.at[w, pl.ds(pl.multiple_of(t * chunk, 16), chunk), :],
                              w1.at[w, o - 1], wsnd.at[w, o - 1], wrcv.at[w, o - 1], peer, ty))
        return cps

    def second(w, cps):
        n = 2 * (ny if w else nx)
        chunk = chans // n
        m = (cy if w else cx) * 2 + core
        acc = wsum[w, pl.ds(pl.multiple_of(m * chunk, 16), chunk), :]
        for o, cp in enumerate(cps):
            cp.wait_recv()
            acc = acc + w1[w, o].astype(F32)
        n2 = nx if w else ny
        third = sz.taps // 3
        for s in range(n2):
            parts = [acc[s * span:(s + 1) * span, g * third:(g + 1) * third] for g in range(3)]
            if sz.pack > 3 * span:
                parts.append(jnp.zeros((sz.pack - 3 * span, third), F32))
            wst2[w, s] = jnp.concatenate(parts, axis=0).astype(BF16)
        mine = cx if w else cy
        nxt = []
        for o in range(1, n2):
            t = (mine + o) % n2
            peer = ((t * ny + cy) if w else (cx * ny + t)) * 2 + core
            nxt.append(remote(wst2.at[w, t], w2.at[w, o - 1],
                              wsnd.at[w, 8 + o], wrcv.at[w, 8 + o], peer, ty))
        return nxt

    def last(w, cps):
        mine = cx if w else cy
        acc = wst2[w, mine].astype(F32)
        for o, cp in enumerate(cps):
            cp.wait_recv()
            acc = acc + w2[w, o].astype(F32)
        w3[w, ty] = acc
        nxt = []
        for o in range(1, gy):
            nxt.append(remote(w3.at[w, ty], w3.at[w, ty], wsnd.at[w, 12 + o], wrcv.at[w, 12 + o],
                              tx, (ty + o) % gy))
        return nxt

    def finish(w, cps, dst):
        for cp in cps:
            cp.wait_recv()
        acc = w3[w, 0]
        for z in range(1, gy):
            acc = acc + w3[w, z]
        for g in range(3):
            for u in range(3):
                dst[3 * g + u] = acc[g * span:(g + 1) * span, u * chans:(u + 1) * chans]

    weight_grad(1, cot_t, lambda d: a_act[d * cols:d * cols + npx, :])
    sb = first(1)

    def turn_bp(i, _):
        q = pl.multiple_of(i * pc, 128)
        bp_t[:, pl.ds(q, pc)] = lax.dot_general(
            perm_a, a_bp[pl.ds(pl.multiple_of(q + cols, cols), pc), chans:2 * chans], NT,
            preferred_element_type=F32).astype(BF16)
        return 0
    lax.fori_loop(0, px // pc, turn_bp, 0)
    weight_grad(0, bp_t, lambda d: a_field[d + 1:d + 1 + rows, 0:cols, :].reshape(npx, 3 * chans))
    sa = first(0)

    def coarse_body(i, acc):
        q = pl.multiple_of(i * pc, 128)
        bf = (cot_v[pl.ds(q, pc), :].astype(F32) + conv_main(a_bp, wat, i * cm, cm)).astype(BF16)
        br = lax.dot_general(lift_v[...], bf, NT, preferred_element_type=F32).astype(BF16)
        return acc + jnp.dot(br, interp2[pl.ds(q, pc), :], preferred_element_type=F32)
    bb = lax.fori_loop(0, px // pc, coarse_body, jnp.zeros((chans_in, listed * cells), F32))
    for k in range(listed):
        v = bb[:, k * cells:(k + 1) * cells]
        gsum[k] = v
        gsend[k] = v.astype(BF16)
    d1 = [remote(gsend, g1.at[1], gsnd.at[0], grcv.at[0], tx, down),
          remote(gsend, g1.at[0], gsnd.at[1], grcv.at[1], tx, up)]

    sb = second(1, sb)
    sa = second(0, sa)

    def out_body(i, _):
        q = pl.multiple_of(i * pc, 128)
        out_v[pl.ds(q, pc), :] = (field[pl.ds(q, pc), :].astype(F32)
                                  + conv_main(a_act, wb_v, i * cm, cm)).astype(BF16)
        return 0
    lax.fori_loop(0, px // pc, out_body, 0)
    st_out = local(out_v, out, 7)

    for cp in d1:
        cp.wait_recv()
    cand = [(ids[k], lambda k=k: gsum[k]) for k in range(listed)]
    for s in range(2):
        for k in range(listed):
            cand.append((lsm[s, k, 0], lambda s=s, k=k: g1[s, k].astype(F32)))

    def spread(dx, m):
        want = ((tx + dx) * gy + ty) * nb + m
        acc = jnp.zeros((chans_in, cells), F32)
        for i, get in cand:
            acc = acc + jnp.where(i == want, get(), 0.0)
        return acc

    d2 = []
    for s, dx, to in ((0, -1, left), (1, 1, right)):
        def body(m, _):
            g2send[s, m] = spread(dx, m).astype(BF16)
            return 0
        lax.fori_loop(0, nb, body, 0)
        d2.append(remote(g2send.at[s], g2.at[1 - s], gsnd.at[2 + s], grcv.at[2 + s], to, ty))

    def own(m, _):
        gacc[m] = spread(0, m)
        return 0
    lax.fori_loop(0, nb, own, 0)

    sb = last(1, sb)
    sa = last(0, sa)
    finish(1, sb, gb)
    finish(0, sa, ga)
    for cp in d2:
        cp.wait_recv()

    def total(m, _):
        gc[m] = gacc[m] + g2[0, m].astype(F32) + g2[1, m].astype(F32)
        return 0
    lax.fori_loop(0, nb, total, 0)
    st_out.wait()
    for cp in started:
        cp.wait_send()


def fused(sz, lists, coarse, interp, fine, lift, wa, wb, cot):
    rows, cols, chans, px, width, ext = sz.rows, sz.cols, sz.chans, sz.px, sz.width, sz.ext
    nb, ci, cells, listed = sz.blocks, sz.chans_in, sz.cells, sz.listed
    n1 = 2 * max(sz.nx, sz.ny) - 1
    n2 = max(sz.nx, sz.ny)
    chunk = chans // (2 * min(sz.nx, sz.ny))
    vm = pltpu.VMEM
    dma = pltpu.SemaphoreType.DMA
    anyspace = pl.BlockSpec(memory_space=pl.ANY)
    vspace = pl.BlockSpec(memory_space=pltpu.VMEM)
    x = vm(((rows + 4) * width, chans), F32)
    a_ext = vm((rows + 4, ext, 3 * chans), BF16)
    a_main = vm(((rows + 2) * cols, 3 * chans), BF16)
    scratch = [
        vm((3, nb, ci, cells), BF16), vm((8, 128), jnp.int32), vm((2, 8, 128), jnp.int32),
        pltpu.SMEM((2, 8, 128), jnp.int32), vm((2, listed, ci, cells), BF16),
        vm((3, listed, ci, cells), BF16),
        vm((px * listed, cells), BF16), vm((px * listed // 8, cells), F32),
        vm((px, listed * cells), BF16), vm((px, chans), BF16), vm((ci, chans), BF16),
        vm((9 * chans, chans), BF16), vm((9 * chans, chans), BF16),
        vm((9 * chans, chans), BF16), vm((9 * chans, chans), BF16),
        vm((px, chans), BF16), vm((listed * cells, ci), BF16),
        x, x, x, x, a_ext, a_ext, a_main, a_main,
        vm(((rows + 2) * ext, chans), F32), vm((px, chans), BF16), vm((px, chans), BF16),
        vm((chans, px), BF16), vm((chans, px), BF16),
        vm((2, 2, 2 * rows, chans), BF16), vm((2, 4, 16, chans), BF16),
        vm((2, 2, 2 * cols, chans), BF16), vm((2, 2, 2 * rows, chans), BF16),
        vm((2, 4, 16, chans), BF16),
        vm((2, chans, 9 * chans), F32), vm((2, chans, 9 * chans), BF16),
        vm((2, n1, chunk, 9 * chans), BF16),
        vm((2, n2, sz.pack, 3 * chans), BF16), vm((2, n2 - 1, sz.pack, 3 * chans), BF16),
        vm((2, sz.gy, sz.pack, 3 * chans), F32),
        vm((listed, ci, cells), F32), vm((listed, ci, cells), BF16), vm((2, listed, ci, cells), BF16),
        vm((2, nb, ci, cells), BF16), vm((2, nb, ci, cells), BF16), vm((nb, ci, cells), F32),
        dma((8,)), dma, dma((6,)), dma((6,)), dma((2, 8)), dma((2, 8)),
        dma((2, 16)), dma((2, 16)), dma((4,)), dma((4,)),
    ]
    flops = 2 * px * (6 * 9 * chans * chans + 2 * listed * cells * ci + 2 * ci * chans)
    return pl.pallas_call(
        functools.partial(kernel, sz),
        out_shape=(
            jax.ShapeDtypeStruct((px, chans), BF16),
            jax.ShapeDtypeStruct((9, sz.span, chans), F32),
            jax.ShapeDtypeStruct((9, sz.span, chans), F32),
            jax.ShapeDtypeStruct((nb, ci, cells), F32),
        ),
        in_specs=[pl.BlockSpec(memory_space=pltpu.SMEM)] + [anyspace] * 7,
        out_specs=(anyspace, vspace, vspace, vspace),
        scratch_shapes=scratch,
        compiler_params=pltpu.CompilerParams(
            collective_id=0, has_side_effects=True, vmem_limit_bytes=56 * MIB),
        cost_estimate=pl.CostEstimate(flops=flops, bytes_accessed=5 * MIB, transcendentals=px * chans),
    )(lists, coarse, interp, fine, lift, wa, wb, cot)


def on_device(nx, ny, coarse, lists, interp, fine_own, lift, conv_a, conv_b, cotangent):
    rows, cols, chans = fine_own.shape
    listed, cells = interp.shape[2:]
    blocks, chans_in = coarse.shape[2:4]
    sz = Sizes(lax.axis_size("gx"), lax.axis_size("gy"), nx, ny, rows, cols, chans, chans_in,
               cells, listed, blocks)
    output, ga, gb, gc = fused(
        sz,
        lists.reshape(1, listed),
        coarse.reshape(blocks, chans_in, cells),
        interp.reshape(rows * cols * listed, cells),
        fine_own.reshape(rows * cols, chans),
        lift,
        conv_a.reshape(9 * chans, chans),
        conv_b.reshape(9 * chans, chans),
        cotangent.reshape(rows * cols, chans),
    )
    return (
        output.reshape(rows, cols, chans),
        jnp.transpose(ga, (0, 2, 1)),
        jnp.transpose(gb, (0, 2, 1)),
        gc.reshape(1, 1, blocks, chans_in, cells),
    )


def solution(mesh):
    side = {32: 4, 8: 2}[mesh.shape["gx"]]
    placed = (
        P("gx", "gy", None, None, None),
        P("gx", "gy", None),
        P("gx", "gy", None, None),
        P("gx", "gy", None),
        P(),
        P(),
        P(),
        P("gx", "gy", None),
    )
    return jax.shard_map(
        functools.partial(on_device, side, side),
        mesh=mesh,
        in_specs=placed,
        out_specs=(
            P("gx", "gy", None),
            P(None, None, "gx"),
            P(None, None, "gx"),
            P("gx", "gy", None, None, None),
        ),
        check_vma=False,
    )
```

time: 313 us -> 62.9 us (0.20)
  waiting for transfers between devices: 154 us -> 0 us
  starting transfers between devices: 64 us -> 0 us
  Pallas kernels: 0 us -> 55.7 us
  matrix products: 35.1 us -> 0 us
  local copies, waits for them, and re-layouts: 31.5 us -> 6.2 us
  between operations: 15 us -> 0.64 us
  other arithmetic: 11.3 us -> 0 us
    psum x1 -> x0, waiting for transfers between devices: 141 us -> none  [on_device(): total_a, total_b = lax.psum((partial_a, partial_b), ('gx', 'gy'))]
    ppermute x24 -> x0, starting transfers between devices: 63.9 us -> none  [the longest x12 48.1 us: with_halo(): lax.ppermute(lax.slice_in_dim(block, block.shape[dim] - width, None, axis...]
    pallas_call x0 -> x1, Pallas kernels: none -> 55.7 us  [fused(): pl.pallas_call(functools.partial(kernel, sz), out_shape=(jax.ShapeDtypeSt...]
    dot_general x58 -> x0, matrix products: 35.1 us -> none  [the longest x18 11.8 us: weight_grad(): lax.dot_general(piece, flat, (((0,), (0,)), ((), ())), preferred_element_...]
    ppermute x24 -> x0, waiting for transfers between devices: 13.5 us -> none  [the longest x12 11.7 us: with_halo(): lax.ppermute(lax.slice_in_dim(block, 0, width, axis=dim), axis, backward)]
    slice x14 -> x0, local copies, waits for them, and re-layouts: 9.95 us -> none  [the longest x3 3.41 us: conv_valid(): padded[1 + di:1 + di + rows, 1 + dj:1 + dj + cols].reshape(-1, chans)]
    unnamed x70 -> x4, local copies, waits for them, and re-layouts: 15 us -> 6.2 us
    concatenate x7 -> x0, other arithmetic: 5.41 us -> none  [with_halo(): block = jnp.concatenate([low, block, high], axis=dim)]
  transfers between devices with their start and end apart: 25 -> 0, of which waited for: 6 -> 0; matrix products, arithmetic and copies ran while one was open for 12% -> 0% of each run, Pallas kernels for 0% -> 0%
where the time goes in v1:
time: 62.9 us; the launch traced here: 62.6 us
  Pallas kernels  55.7 us (89%)
  local copies, waits for them, and re-layouts  6.2 us (10%)
  between operations  0.64 us (1%)
    pallas_call x1, Pallas kernels, fused(): pl.pallas_call(functools.partial(kernel, sz), out_shape=(jax.ShapeDtypeSt...  55.7 us
    unnamed x4, local copies, waits for them, and re-layouts  6.2 us

profile of v1, /device:TPU:0, one launch (start us, length us, event | category | flops | bytes accessed | tf_op | source)
XLA Modules:
  0.0 62.6 jit_solution(16016445346884972194)
XLA Ops:
  0.6 55.7 %shard_map.111 = (bf16[2048,128]{1,0:T(8,128)(2,1)}, f32[9,4,128]{2,1,0:T(4,128)}, f32[9,4,128]{2,1,0:T(4,128)}, f32[8,64,128]{2,1,0:T(8,128)}) custom-call(s32[1,4]{1,0:T(1,128)} %bitcast.21, bf16[8,64,128]{2,1,0:T(8,128)(2,1)} %bitcast.20, bf16[8192,128]{1,0:T(8,128)(2,1)} %bitcast.15, bf16[2048,128]{1,0:T(8,128)(2,1)} %bitcast.16, bf16[64,128]{1,0:T(8,128)(2,1)} %lift.1, ...), custom_call_target="tpu_custom_call" | custom-call | flops 3959422976 | bytes 5242880 | tf_op jit(solution)/shard_map/pallas_call | solution.py:506
  56.4 1.9 %copy.16 = bf16[32,64,128]{2,1,0:T(8,128)(2,1)} copy(bf16[32,64,128]{2,1,0:T(8,128)(2,1)} %bitcast.11) | data formatting | bytes 1048576
  58.2 1.3 %copy.17 = f32[9,128,4]{1,2,0:T(4,128)} copy(f32[9,128,4]{1,2,0:T(4,128)} %bitcast.14) | data formatting | bytes 36864
  59.6 1.3 %copy.18 = f32[9,128,4]{1,2,0:T(4,128)} copy(f32[9,128,4]{1,2,0:T(4,128)} %bitcast.13) | data formatting | bytes 36864
  60.9 1.7 %copy.19 = f32[1,1,8,64,128]{4,3,2,1,0:T(8,128)} copy(f32[1,1,8,64,128]{4,3,2,1,0:T(8,128)} %bitcast.12) | data formatting | bytes 524288

commit v2 on v1

v2 whole, which is shorter than its diff:
```python
import functools

import jax
import jax.numpy as jnp
from jax import lax
from jax.experimental import pallas as pl
from jax.experimental.pallas import tpu as pltpu
from jax.sharding import PartitionSpec as P

MESH = pl.DeviceIdType.MESH
F32 = jnp.float32
BF16 = jnp.bfloat16
MIB = 1024 * 1024
NT = (((1,), (1,)), ((), ()))
AROUND = ((-1, 0), (1, 0), (0, -1), (0, 1), (-1, -1), (1, 1), (-1, 1), (1, -1))


class Sizes:
    def __init__(self, gx, gy, nx, ny, rows, cols, chans, chans_in, cells, listed, blocks):
        self.gx, self.gy, self.nx, self.ny = gx, gy, nx, ny
        self.rows, self.cols = rows, cols
        self.chans, self.chans_in, self.cells = chans, chans_in, cells
        self.listed, self.blocks = listed, blocks
        self.px = rows * cols
        self.width = cols + 32
        self.span = chans // gx
        self.pack = -(-3 * self.span // 16) * 16
        self.plane = nx * ny


def kernel(
    sz,
    lists, coarse, interp, fine, lift, wa, wb, cot,
    out, ga, gb, gc,
    call, lvec, lrecv, lsm, picked, crecv,
    raw, rawf, interp2, fine_v, lift_v, wa_v, wb_v, wat, wbt, w2_a, w2_b, w2_at, w2_bt, cot_v, bt,
    x_cot, x_field, x_act, x_bp, a_cot, a_field, s_cot, s_field, a_act, a_bp,
    ba_main, ba_strip, field, out_v, cot_t, bp_t,
    hs_cols, hs_corner, hr_rows, hr_cols, hr_corner,
    wsum, wsend, w1, wst2, w2, w3,
    gsum, gsend, g1,
    local_sem, lsem, csend, crcv, hsend, hrcv, wsnd, wrcv, gsnd, grcv,
):
    tx = lax.axis_index("gx")
    ty = lax.axis_index("gy")
    gx, gy, nx, ny = sz.gx, sz.gy, sz.nx, sz.ny
    rows, cols, chans, width, px = sz.rows, sz.cols, sz.chans, sz.width, sz.px
    listed, cells, chans_in, nb, span = sz.listed, sz.cells, sz.chans_in, sz.blocks, sz.span
    core = tx % 2
    mine = tx // 2
    around = [((tx + dx + gx) % gx, (ty + dy + gy) % gy) for dx, dy in AROUND]
    started = []

    def remote(src, dst, ssem, rsem, px_, py_):
        copy = pltpu.make_async_remote_copy(
            src_ref=src, dst_ref=dst, send_sem=ssem, recv_sem=rsem,
            device_id=(px_, py_), device_id_type=MESH,
        )
        copy.start()
        started.append(copy)
        return copy

    def local(src, dst, i):
        copy = pltpu.make_async_copy(src, dst, local_sem.at[i])
        copy.start()
        return copy

    ld_coarse = local(coarse, call.at[1], 0)
    ld_cot = local(cot, cot_v, 1)
    ld_wb = local(wb, wb_v, 3)
    ld_raw = local(interp, raw, 2)
    ld_wa = local(wa, wa_v, 4)
    ld_fine = local(fine, fine_v, 5)
    ld_lift = local(lift, lift_v, 6)

    peers = list(around)
    for o in range(2, gy - 1):
        peers.append((tx, (ty + o) % gy))
    for o in range(1, sz.plane):
        peers.append((((mine + o) % sz.plane) * 2 + core, ty))
    barrier = pltpu.get_barrier_semaphore()
    for p in peers:
        pl.semaphore_signal(barrier, inc=1, device_id=p, device_id_type=MESH)
    rowi = lax.broadcasted_iota(jnp.int32, (8, 128), 0)
    vec = jnp.zeros((8, 128), jnp.int32)
    for k in range(listed):
        vec = jnp.where(rowi == k, lists[0, k], vec)
    lvec[...] = vec
    ld_coarse.wait()
    ld_cot.wait()

    def fill(x, src):
        for r in range(rows):
            x[(r + 2) * width + 16:(r + 2) * width + 16 + cols, :] = src[
                r * cols:(r + 1) * cols].astype(F32)

    fill(x_cot, cot_v)
    pl.semaphore_wait(barrier, len(peers))

    c1 = [remote(call.at[1], call.at[2], csend.at[0], crcv.at[0], *around[0]),
          remote(call.at[1], call.at[0], csend.at[1], crcv.at[1], *around[1])]
    l1 = [None] * 8
    for i in (2, 3, 0, 1, 4, 5, 6, 7):
        l1[i] = remote(lvec, lrecv.at[i ^ 1], csend.at[4 + i], crcv.at[4 + i], *around[i])

    def rim_send(e, x, main):
        cps = []
        n2 = 2 * cols
        cps.append(remote(main.at[pl.ds(0, n2), :], hr_rows.at[e, 1],
                          hsend.at[e, 0], hrcv.at[e, 0], *around[0]))
        cps.append(remote(main.at[pl.ds(px - n2, n2), :], hr_rows.at[e, 0],
                          hsend.at[e, 1], hrcv.at[e, 1], *around[1]))
        for s, c0 in ((0, 0), (1, cols - 2)):
            for j in range(2):
                hs_cols[e, s, j * rows:(j + 1) * rows, :] = x[
                    pl.ds(2 * width + 16 + c0 + j, rows, stride=width), :].astype(BF16)
        cps.append(remote(hs_cols.at[e, 0], hr_cols.at[e, 1],
                          hsend.at[e, 2], hrcv.at[e, 2], *around[2]))
        cps.append(remote(hs_cols.at[e, 1], hr_cols.at[e, 0],
                          hsend.at[e, 3], hrcv.at[e, 3], *around[3]))
        q = 0
        for r0, i0 in ((0, (4, 6)), (rows - 2, (7, 5))):
            for c0, i in ((0, i0[0]), (cols - 2, i0[1])):
                parts = [x[(2 + r0 + i_) * width + 16 + c0:(2 + r0 + i_) * width + 18 + c0, :]
                         for i_ in range(2)]
                parts.append(jnp.zeros((12, chans), F32))
                hs_corner[e, q] = jnp.concatenate(parts, axis=0).astype(BF16)
                cps.append(remote(hs_corner.at[e, q], hr_corner.at[e, 3 - q],
                                  hsend.at[e, 4 + q], hrcv.at[e, 4 + q], *around[i]))
                q += 1
        return cps

    in_x = (tx > 0, tx < gx - 1)
    in_y = (ty > 0, ty < gy - 1)

    def rim_take(e, x, cps):
        for cp in cps:
            cp.wait_recv()
        for s, r0 in ((0, 0), (1, rows + 2)):
            v = jnp.where(in_x[s], hr_rows[e, s].astype(F32), 0.0)
            for i in range(2):
                x[(r0 + i) * width + 16:(r0 + i) * width + 16 + cols, :] = v[i * cols:(i + 1) * cols]
        for s, c0 in ((0, 14), (1, 16 + cols)):
            v = jnp.where(in_y[s], hr_cols[e, s].astype(F32), 0.0)
            for j in range(2):
                x[pl.ds(2 * width + c0 + j, rows, stride=width), :] = v[j * rows:(j + 1) * rows]
        q = 0
        for sr, r0 in ((0, 0), (1, rows + 2)):
            for sc, c0 in ((0, 14), (1, 16 + cols)):
                v = jnp.where(jnp.logical_and(in_x[sr], in_y[sc]),
                              hr_corner[e, q].astype(F32), 0.0)
                for i in range(2):
                    x[(r0 + i) * width + c0:(r0 + i) * width + c0 + 2, :] = v[2 * i:2 * i + 2]
                q += 1

    def widen(x, a, first, last, shift):
        for r in range(first, last):
            for dj in range(3):
                c = r * width + 15 + dj
                a[(r - shift) * cols:(r - shift + 1) * cols, dj * chans:(dj + 1) * chans] = x[
                    c:c + cols, :].astype(BF16)

    def widen_edge(x, a, first, last):
        for r in range(first, last):
            c = r * width + 15
            a[r * cols:r * cols + 16, 0:chans] = x[c:c + 16, :].astype(BF16)
            c = r * width + 17 + cols - 16
            a[(r + 1) * cols - 16:(r + 1) * cols, 2 * chans:3 * chans] = x[c:c + 16, :].astype(BF16)

    def widen_strip(x, s):
        for r in range(rows + 4):
            for dj in range(3):
                c = r * width + 15 + dj
                v = jnp.concatenate(
                    [x[c + cols - 4:c + cols + 4, :], x[c - 4:c + 4, :]], axis=0)
                s[r * 16:(r + 1) * 16, dj * chans:(dj + 1) * chans] = v.astype(BF16)

    def conv_pairs(a, w2x, first, pairs):
        v = jnp.concatenate([
            jnp.concatenate([a[(first + 2 * p + d) * cols:(first + 2 * p + d + 1) * cols, :]
                             for p in range(pairs)], axis=0) for d in range(4)], axis=1)
        res = jnp.dot(v, w2x[...], preferred_element_type=F32)
        return [(first + 2 * p + s, res[p * cols:(p + 1) * cols, s * chans:(s + 1) * chans])
                for p in range(pairs) for s in range(2)]

    def conv_strip(s, w):
        v = jnp.concatenate([s[d * 16:(d + rows + 2) * 16, :] for d in range(3)], axis=1)
        return jnp.dot(v, w[...], preferred_element_type=F32)

    h_cot = rim_send(0, x_cot, cot_v)

    third = 3 * chans
    ld_wb.wait()
    ld_wa.wait()
    for src, flip, two, two_flip in ((wb_v, wbt, w2_b, w2_bt), (wa_v, wat, w2_a, w2_at)):
        for t in range(9):
            flip[t * chans:(t + 1) * chans, :] = src[
                (8 - t) * chans:(9 - t) * chans, :].astype(F32).T.astype(BF16)
        for one, both in ((src, two), (flip, two_flip)):
            both[0:3 * third, 0:chans] = one[...]
            both[third:4 * third, chans:2 * chans] = one[...]
            both[3 * third:4 * third, 0:chans] = jnp.zeros((third, chans), BF16)
            both[0:third, chans:2 * chans] = jnp.zeros((third, chans), BF16)

    ld_raw.wait()
    step = px // 8

    def relay(i, _):
        rawf[...] = raw[pl.ds(pl.multiple_of(i * step * listed, 16), step * listed), :].astype(F32)
        for k in range(listed):
            interp2[pl.ds(pl.multiple_of(i * step, 16), step), k * cells:(k + 1) * cells] = rawf[
                pl.ds(k, step, stride=listed), :].astype(BF16)
        return 0
    lax.fori_loop(0, 8, relay, 0)

    ri = lax.broadcasted_iota(jnp.int32, (chans, chans), 0)
    ci = lax.broadcasted_iota(jnp.int32, (chans, chans), 1)
    half = chans // 2
    rest = ri % half
    perm = jnp.where(
        ci == (rest // span) * 2 * span + (ri // half) * span + rest % span, 1.0, 0.0).astype(BF16)
    cot_t[...] = lax.dot_general(perm, cot_v[...], NT, preferred_element_type=F32).astype(BF16)

    for cp in c1 + l1[2:4]:
        cp.wait_recv()
    ld_l = pltpu.make_async_copy(lrecv.at[pl.ds(2, 2)], lsm.at[pl.ds(2, 2)], lsem.at[0])
    ld_l.start()
    ld_l.wait()

    def clip(v):
        return jnp.minimum(jnp.maximum(v, 0), 2)

    c2 = []
    for s in (2, 3):
        for k in range(listed):
            i = lsm[s, k, 0]
            picked[s - 2, k] = call[clip(i // (nb * gy) - tx + 1), i % nb]
        c2.append(remote(picked.at[s - 2], crecv.at[3 - s], csend.at[s], crcv.at[s], *around[s]))
    ids = [lists[0, k] for k in range(listed)]
    for k in range(listed):
        i = ids[k]
        crecv[2, k] = call[clip(i // (nb * gy) - tx + 1), i % nb]

    rim_take(0, x_cot, h_cot)
    widen(x_cot, a_cot, 0, rows + 4, 0)
    widen_strip(x_cot, s_cot)
    for r, v in conv_pairs(a_cot, w2_bt, 0, (rows + 2) // 2):
        ba_main[r * cols:(r + 1) * cols, :] = v
    ba_strip[...] = conv_strip(s_cot, wbt)

    for cp in c2:
        cp.wait_recv()
    for k in range(listed):
        oy = (ids[k] // nb) % gy
        which = jnp.where(oy == ty, 2, jnp.where(oy < ty, 0, 1))
        bt[k * cells:(k + 1) * cells, :] = crecv[which, k].astype(F32).T.astype(BF16)
    ld_fine.wait()
    ld_lift.wait()
    g = jnp.dot(interp2[...], bt[...], preferred_element_type=F32).astype(BF16)
    f = fine_v[...].astype(F32) + jnp.dot(g, lift_v[...], preferred_element_type=F32)
    f = f.astype(BF16)
    field[...] = f
    fill(x_field, f)

    h_field = rim_send(1, x_field, field)
    widen(x_field, a_field, 2, rows + 2, 0)

    def point(pre, back):
        sig = 1.0 / (1.0 + jnp.exp(-pre))
        return pre * sig, back * (sig * (1.0 + pre * (1.0 - sig)))

    def keep(r, pre):
        act, bp = point(pre, ba_main[r * cols:(r + 1) * cols, :])
        c = (r + 1) * width + 16
        x_act[c:c + cols, :] = act
        x_bp[c:c + cols, :] = bp

    for r, pre in conv_pairs(a_field, w2_a, 2, (rows - 2) // 2):
        keep(r, pre)

    rim_take(1, x_field, h_field)
    widen(x_field, a_field, 0, 2, 0)
    widen(x_field, a_field, rows + 2, rows + 4, 0)
    widen_edge(x_field, a_field, 2, rows + 2)
    widen_strip(x_field, s_field)
    for r0 in (0, rows):
        for r, pre in conv_pairs(a_field, w2_a, r0, 1):
            keep(r, pre)
    pre = conv_strip(s_field, wa_v)
    act, bp = point(pre, ba_strip[...])
    inside = lax.broadcasted_iota(jnp.int32, (8, chans), 0)
    far = jnp.logical_or(inside < 4, in_y[1])
    near = jnp.logical_or(inside >= 4, in_y[0])
    for x, v in ((x_act, act), (x_bp, bp)):
        for r in range(rows + 2):
            c = (r + 1) * width + 16
            x[c + cols - 4:c + cols + 4, :] = jnp.where(far, v[r * 16:r * 16 + 8], 0.0)
            x[c - 4:c + 4, :] = jnp.where(near, v[r * 16 + 8:r * 16 + 16], 0.0)

    for ok, r in ((in_x[0], 1), (in_x[1], rows + 2)):
        @pl.when(jnp.logical_not(ok))
        def _():
            for x in (x_act, x_bp):
                x[r * width:(r + 1) * width, :] = jnp.zeros((width, chans), F32)

    def weight_grad(w, lhs, a, first):
        v = jnp.concatenate([a[(first + d) * cols:(first + d) * cols + px, :] for d in range(3)],
                            axis=1)
        g = jnp.dot(lhs, v, preferred_element_type=F32)
        wsum[w] = g
        wsend[w] = g.astype(BF16)

    def first(w):
        other = 1 - core
        return remote(wsend.at[w, pl.ds(pl.multiple_of(other * half, 16), half), :],
                      w1.at[w], wsnd.at[w, 0], wrcv.at[w, 0], mine * 2 + other, ty)

    def second(w, cp):
        own = wsum[w, pl.ds(pl.multiple_of(core * half, 16), half), :]
        cp.wait_recv()
        acc = own + w1[w].astype(F32)
        for s in range(sz.plane):
            parts = [acc[s * span:(s + 1) * span, g * third:(g + 1) * third] for g in range(3)]
            if sz.pack > 3 * span:
                parts.append(jnp.zeros((sz.pack - 3 * span, third), F32))
            wst2[w, s] = jnp.concatenate(parts, axis=0).astype(BF16)
        nxt = []
        for o in range(1, sz.plane):
            t = (mine + o) % sz.plane
            nxt.append(remote(wst2.at[w, t], w2.at[w, o - 1],
                              wsnd.at[w, o], wrcv.at[w, o], t * 2 + core, ty))
        return nxt

    def last(w, cps):
        acc = wst2[w, mine].astype(F32)
        for o, cp in enumerate(cps):
            cp.wait_recv()
            acc = acc + w2[w, o].astype(F32)
        w3[w, ty] = acc
        nxt = []
        for o in range(1, gy):
            j = sz.plane + o
            nxt.append(remote(w3.at[w, ty], w3.at[w, ty], wsnd.at[w, j], wrcv.at[w, j],
                              tx, (ty + o) % gy))
        return nxt

    def finish(w, cps, dst):
        for cp in cps:
            cp.wait_recv()
        acc = w3[w, 0]
        for z in range(1, gy):
            acc = acc + w3[w, z]
        for g in range(3):
            for u in range(3):
                dst[3 * g + u] = acc[g * span:(g + 1) * span, u * chans:(u + 1) * chans]

    widen(x_act, a_act, 1, rows + 3, 1)
    weight_grad(1, cot_t[...], a_act, 0)
    sb = first(1)
    widen(x_bp, a_bp, 1, rows + 3, 1)
    bp_t[...] = lax.dot_general(
        perm, a_bp[cols:cols + px, chans:2 * chans], NT, preferred_element_type=F32).astype(BF16)
    weight_grad(0, bp_t[...], a_field, 1)
    sa = first(0)
    sb = second(1, sb)

    bf = [(cot_v[r * cols:(r + 1) * cols, :].astype(F32) + v).astype(BF16)
          for r, v in conv_pairs(a_bp, w2_at, 0, rows // 2)]
    br = lax.dot_general(lift_v[...], jnp.concatenate(bf, axis=0), NT,
                         preferred_element_type=F32).astype(BF16)
    sa = second(0, sa)
    bb = jnp.dot(br, interp2[...], preferred_element_type=F32)
    for k in range(listed):
        v = bb[:, k * cells:(k + 1) * cells]
        gsum[k] = v
        gsend[k] = v.astype(BF16)
    d1 = [remote(gsend, g1.at[i ^ 1], gsnd.at[i], grcv.at[i], *around[i]) for i in range(8)]

    for r, v in conv_pairs(a_act, w2_b, 0, rows // 2):
        q = slice(r * cols, (r + 1) * cols)
        out_v[q, :] = (field[q, :].astype(F32) + v).astype(BF16)
    st_out = local(out_v, out, 7)

    sb = last(1, sb)
    sa = last(0, sa)
    for i in (0, 1, 4, 5, 6, 7):
        l1[i].wait_recv()
    ld_m = [pltpu.make_async_copy(lrecv.at[pl.ds(i, n)], lsm.at[pl.ds(i, n)], lsem.at[j])
            for j, (i, n) in ((1, (0, 2)), (2, (4, 4)))]
    for cp in ld_m:
        cp.start()
    for cp in ld_m:
        cp.wait()
    for cp in d1:
        cp.wait_recv()
    cand = [(ids[k], lambda k=k: gsum[k]) for k in range(listed)]
    for s in range(8):
        for k in range(listed):
            cand.append((lsm[s, k, 0], lambda s=s, k=k: g1[s, k].astype(F32)))
    base = (tx * gy + ty) * nb

    def total(m, _):
        acc = jnp.zeros((chans_in, cells), F32)
        for i, get in cand:
            acc = acc + jnp.where(i == base + m, get(), 0.0)
        gc[m] = acc
        return 0
    lax.fori_loop(0, nb, total, 0)
    finish(1, sb, gb)
    finish(0, sa, ga)
    st_out.wait()
    for cp in started:
        cp.wait_send()


def hand_out(*refs):
    count = (len(refs) - 1) // 2
    sems = refs[-1]
    copies = [pltpu.make_async_copy(refs[i], refs[count + i], sems.at[i]) for i in range(count)]
    for cp in copies:
        cp.start()
    for cp in copies:
        cp.wait()


def fused(sz, lists, coarse, interp, fine, lift, wa, wb, cot):
    rows, cols, chans, px, width = sz.rows, sz.cols, sz.chans, sz.px, sz.width
    nb, ci, cells, listed = sz.blocks, sz.chans_in, sz.cells, sz.listed
    vm = pltpu.VMEM
    dma = pltpu.SemaphoreType.DMA
    anyspace = pl.BlockSpec(memory_space=pl.ANY)
    vspace = pl.BlockSpec(memory_space=pltpu.VMEM)
    x = vm(((rows + 4) * width, chans), F32)
    a_ext = vm(((rows + 4) * cols, 3 * chans), BF16)
    strip = vm(((rows + 4) * 16, 3 * chans), BF16)
    a_main = vm(((rows + 2) * cols, 3 * chans), BF16)
    w = vm((9 * chans, chans), BF16)
    w2 = vm((12 * chans, 2 * chans), BF16)
    scratch = [
        vm((3, nb, ci, cells), BF16), vm((8, 128), jnp.int32), vm((8, 8, 128), jnp.int32),
        pltpu.SMEM((8, 8, 128), jnp.int32), vm((2, listed, ci, cells), BF16),
        vm((3, listed, ci, cells), BF16),
        vm((px * listed, cells), BF16), vm((px * listed // 8, cells), F32),
        vm((px, listed * cells), BF16), vm((px, chans), BF16), vm((ci, chans), BF16),
        w, w, w, w, w2, w2, w2, w2,
        vm((px, chans), BF16), vm((listed * cells, ci), BF16),
        x, x, x, x, a_ext, a_ext, strip, strip, a_main, a_main,
        vm(((rows + 2) * cols, chans), F32), vm(((rows + 2) * 16, chans), F32),
        vm((px, chans), BF16), vm((px, chans), BF16),
        vm((chans, px), BF16), vm((chans, px), BF16),
        vm((2, 2, 2 * rows, chans), BF16), vm((2, 4, 16, chans), BF16),
        vm((2, 2, 2 * cols, chans), BF16), vm((2, 2, 2 * rows, chans), BF16),
        vm((2, 4, 16, chans), BF16),
        vm((2, chans, 9 * chans), F32), vm((2, chans, 9 * chans), BF16),
        vm((2, chans // 2, 9 * chans), BF16),
        vm((2, sz.plane, sz.pack, 3 * chans), BF16),
        vm((2, sz.plane - 1, sz.pack, 3 * chans), BF16),
        vm((2, sz.gy, sz.pack, 3 * chans), F32),
        vm((listed, ci, cells), F32), vm((listed, ci, cells), BF16),
        vm((8, listed, ci, cells), BF16),
        dma((8,)), dma((3,)), dma((12,)), dma((12,)), dma((2, 8)), dma((2, 8)),
        dma((2, sz.plane + sz.gy)), dma((2, sz.plane + sz.gy)), dma((8,)), dma((8,)),
    ]
    flops = 2 * px * (6 * 9 * chans * chans + 2 * listed * cells * ci + 2 * ci * chans)
    shapes = (
        jax.ShapeDtypeStruct((px, chans), BF16),
        jax.ShapeDtypeStruct((9, sz.span, chans), F32),
        jax.ShapeDtypeStruct((9, sz.span, chans), F32),
        jax.ShapeDtypeStruct((nb, ci, cells), F32),
    )
    results = pl.pallas_call(
        functools.partial(kernel, sz),
        out_shape=shapes,
        in_specs=[pl.BlockSpec(memory_space=pltpu.SMEM)] + [anyspace] * 7,
        out_specs=(anyspace, vspace, vspace, vspace),
        scratch_shapes=scratch,
        compiler_params=pltpu.CompilerParams(
            collective_id=0, has_side_effects=True, vmem_limit_bytes=56 * MIB),
        cost_estimate=pl.CostEstimate(flops=flops, bytes_accessed=5 * MIB, transcendentals=px * chans),
    )(lists, coarse, interp, fine, lift, wa, wb, cot)
    return pl.pallas_call(
        hand_out,
        out_shape=shapes,
        in_specs=[vspace] * 4,
        out_specs=(anyspace,) * 4,
        scratch_shapes=[dma((4,))],
    )(*results)


def on_device(nx, ny, coarse, lists, interp, fine_own, lift, conv_a, conv_b, cotangent):
    rows, cols, chans = fine_own.shape
    listed, cells = interp.shape[2:]
    blocks, chans_in = coarse.shape[2:4]
    sz = Sizes(lax.axis_size("gx"), lax.axis_size("gy"), nx, ny, rows, cols, chans, chans_in,
               cells, listed, blocks)
    output, ga, gb, gc = fused(
        sz,
        lists.reshape(1, listed),
        coarse.reshape(blocks, chans_in, cells),
        interp.reshape(rows * cols * listed, cells),
        fine_own.reshape(rows * cols, chans),
        lift,
        conv_a.reshape(9 * chans, chans),
        conv_b.reshape(9 * chans, chans),
        cotangent.reshape(rows * cols, chans),
    )
    return (
        output.reshape(rows, cols, chans),
        jnp.transpose(ga, (0, 2, 1)),
        jnp.transpose(gb, (0, 2, 1)),
        gc.reshape(1, 1, blocks, chans_in, cells),
    )


def solution(mesh):
    side = {32: 4, 8: 2}[mesh.shape["gx"]]
    placed = (
        P("gx", "gy", None, None, None),
        P("gx", "gy", None),
        P("gx", "gy", None, None),
        P("gx", "gy", None),
        P(),
        P(),
        P(),
        P("gx", "gy", None),
    )
    return jax.shard_map(
        functools.partial(on_device, side, side),
        mesh=mesh,
        in_specs=placed,
        out_specs=(
            P("gx", "gy", None),
            P(None, None, "gx"),
            P(None, None, "gx"),
            P("gx", "gy", None, None, None),
        ),
        check_vma=False,
    )
```

time: 62.9 us -> 45.7 us (0.73)
  Pallas kernels: 55.7 us -> 44.3 us
  local copies, waits for them, and re-layouts: 6.2 us -> 0 us
    pallas_call x1 -> x2, Pallas kernels: 55.7 us -> 44.3 us  [the longest x1 42.3 us: fused(): pl.pallas_call(functools.partial(kernel, sz), out_shape=shapes, in_specs=...]
    unnamed x4 -> x0, local copies, waits for them, and re-layouts: 6.2 us -> none
where the time goes in v2:
time: 45.7 us; the launch traced here: 45 us
  Pallas kernels  44.3 us (97%)
  between operations  0.64 us (1%)
    pallas_call x1, Pallas kernels, fused(): pl.pallas_call(functools.partial(kernel, sz), out_shape=shapes, in_specs=...  42.3 us
    pallas_call x1, Pallas kernels, fused(): pl.pallas_call(hand_out, out_shape=shapes, in_specs=[vspace] * 4, out_spe...  2.06 us

profile of v2, /device:TPU:0, one launch (start us, length us, event | category | flops | bytes accessed | tf_op | source)
XLA Modules:
  0.0 45.0 jit_solution(10809137912177789432)
XLA Ops:
  0.6 42.3 %shard_map.111 = (bf16[2048,128]{1,0:T(8,128)(2,1)}, f32[9,4,128]{2,1,0:T(4,128)}, f32[9,4,128]{2,1,0:T(4,128)}, f32[8,64,128]{2,1,0:T(8,128)}) custom-call(s32[1,4]{1,0:T(1,128)} %bitcast.21, bf16[8,64,128]{2,1,0:T(8,128)(2,1)} %bitcast.18, bf16[8192,128]{1,0:T(8,128)(2,1)} %bitcast.11, bf16[2048,128]{1,0:T(8,128)(2,1)} %bitcast.12, bf16[64,128]{1,0:T(8,128)(2,1)} %lift.1, ...), custom_call_target="tpu_custom_call" | custom-call | flops 3959422976 | bytes 5242880 | tf_op jit(solution)/shard_map/pallas_call | solution.py:471
  42.9 2.1 %shard_map.112 = (bf16[2048,128]{1,0:T(8,128)(2,1)}, f32[9,4,128]{2,1,0:T(4,128)}, f32[9,4,128]{2,1,0:T(4,128)}, f32[8,64,128]{2,1,0:T(8,128)}) custom-call(bf16[2048,128]{1,0:T(8,128)(2,1)} %get-tuple-element.12.refs_0_, f32[9,4,128]{2,1,0:T(4,128)} %get-tuple-element.13.refs_1_, f32[9,4,128]{2,1,0:T(4,128)} %get-tuple-element.14.refs_2_, ...), custom_call_target="tpu_custom_call" | custom-call | tf_op jit(solution)/shard_map/pallas_call | solution.py:481

commit v3 on v2

--- a/solution.py
+++ b/solution.py
@@ -11,6 +11,7 @@
 F32 = jnp.float32
 BF16 = jnp.bfloat16
 MIB = 1024 * 1024
+PARTS = 2
 NT = (((1,), (1,)), ((), ()))
 AROUND = ((-1, 0), (1, 0), (0, -1), (0, 1), (-1, -1), (1, 1), (-1, 1), (1, -1))
 
@@ -32,14 +33,14 @@
     sz,
     lists, coarse, interp, fine, lift, wa, wb, cot,
     out, ga, gb, gc,
-    call, lvec, lrecv, lsm, picked, crecv,
+    call0, call1, lvec, lrecv, lsm, picked, crecv,
     raw, rawf, interp2, fine_v, lift_v, wa_v, wb_v, wat, wbt, w2_a, w2_b, w2_at, w2_bt, cot_v, bt,
     x_cot, x_field, x_act, x_bp, a_cot, a_field, s_cot, s_field, a_act, a_bp,
-    ba_main, ba_strip, field, out_v, cot_t, bp_t,
+    side_act, side_field, ba_main, ba_strip, field, out_v, cot_t, cot_r,
     hs_cols, hs_corner, hr_rows, hr_cols, hr_corner,
     wsum, wsend, w1, wst2, w2, w3,
     gsum, gsend, g1,
-    local_sem, lsem, csend, crcv, hsend, hrcv, wsnd, wrcv, gsnd, grcv,
+    local_sem, lsem, csend, crcv, c1s, c1r, c2s, c2r, hsend, hrcv, wsnd, wrcv, gsnd, grcv,
 ):
     tx = lax.axis_index("gx")
     ty = lax.axis_index("gy")
@@ -65,7 +66,10 @@
         copy.start()
         return copy
 
-    ld_coarse = local(coarse, call.at[1], 0)
+    calls = (call0, call1)
+    part = chans_in // PARTS
+    cuts = [pl.ds(h * part, part) for h in range(PARTS)]
+    ld_coarse = [local(coarse.at[:, cut], calls[h].at[1], 7 * h) for h, cut in enumerate(cuts)]
     ld_cot = local(cot, cot_v, 1)
     ld_wb = local(wb, wb_v, 3)
     ld_raw = local(interp, raw, 2)
@@ -86,43 +90,35 @@
     for k in range(listed):
         vec = jnp.where(rowi == k, lists[0, k], vec)
     lvec[...] = vec
-    ld_coarse.wait()
-    ld_cot.wait()
 
     def fill(x, src):
         for r in range(rows):
             x[(r + 2) * width + 16:(r + 2) * width + 16 + cols, :] = src[
                 r * cols:(r + 1) * cols].astype(F32)
 
-    fill(x_cot, cot_v)
     pl.semaphore_wait(barrier, len(peers))
 
-    c1 = [remote(call.at[1], call.at[2], csend.at[0], crcv.at[0], *around[0]),
-          remote(call.at[1], call.at[0], csend.at[1], crcv.at[1], *around[1])]
-    l1 = [None] * 8
-    for i in (2, 3, 0, 1, 4, 5, 6, 7):
+    l1 = {}
+
+    def tell(i):
         l1[i] = remote(lvec, lrecv.at[i ^ 1], csend.at[4 + i], crcv.at[4 + i], *around[i])
 
-    def rim_send(e, x, main):
-        cps = []
+    tell(2)
+    tell(3)
+    c1 = [[remote(coarse.at[:, cut], calls[h].at[2 - 2 * i], c1s.at[h, i], c1r.at[h, i], *around[i])
+           for i in range(2)] for h, cut in enumerate(cuts)]
+
+    def rim_rows(e, x, main):
         n2 = 2 * cols
-        cps.append(remote(main.at[pl.ds(0, n2), :], hr_rows.at[e, 1],
-                          hsend.at[e, 0], hrcv.at[e, 0], *around[0]))
-        cps.append(remote(main.at[pl.ds(px - n2, n2), :], hr_rows.at[e, 0],
-                          hsend.at[e, 1], hrcv.at[e, 1], *around[1]))
-        for s, c0 in ((0, 0), (1, cols - 2)):
-            for j in range(2):
-                hs_cols[e, s, j * rows:(j + 1) * rows, :] = x[
-                    pl.ds(2 * width + 16 + c0 + j, rows, stride=width), :].astype(BF16)
-        cps.append(remote(hs_cols.at[e, 0], hr_cols.at[e, 1],
-                          hsend.at[e, 2], hrcv.at[e, 2], *around[2]))
-        cps.append(remote(hs_cols.at[e, 1], hr_cols.at[e, 0],
-                          hsend.at[e, 3], hrcv.at[e, 3], *around[3]))
+        cps = [remote(main.at[pl.ds(0, n2), :], hr_rows.at[e, 1],
+                      hsend.at[e, 0], hrcv.at[e, 0], *around[0]),
+               remote(main.at[pl.ds(px - n2, n2), :], hr_rows.at[e, 0],
+                      hsend.at[e, 1], hrcv.at[e, 1], *around[1])]
         q = 0
         for r0, i0 in ((0, (4, 6)), (rows - 2, (7, 5))):
             for c0, i in ((0, i0[0]), (cols - 2, i0[1])):
-                parts = [x[(2 + r0 + i_) * width + 16 + c0:(2 + r0 + i_) * width + 18 + c0, :]
-                         for i_ in range(2)]
+                parts = [x[(2 + r0 + k) * width + 16 + c0:(2 + r0 + k) * width + 18 + c0, :]
+                         for k in range(2)]
                 parts.append(jnp.zeros((12, chans), F32))
                 hs_corner[e, q] = jnp.concatenate(parts, axis=0).astype(BF16)
                 cps.append(remote(hs_corner.at[e, q], hr_corner.at[e, 3 - q],
@@ -130,16 +126,28 @@
                 q += 1
         return cps
 
+    def rim_cols(e, x):
+        for s, c0 in ((0, 0), (1, cols - 2)):
+            for j in range(2):
+                hs_cols[e, s, j * rows:(j + 1) * rows, :] = x[
+                    pl.ds(2 * width + 16 + c0 + j, rows, stride=width), :].astype(BF16)
+        return [remote(hs_cols.at[e, s], hr_cols.at[e, 1 - s],
+                       hsend.at[e, 2 + s], hrcv.at[e, 2 + s], *around[2 + s]) for s in range(2)]
+
     in_x = (tx > 0, tx < gx - 1)
     in_y = (ty > 0, ty < gy - 1)
 
-    def rim_take(e, x, cps):
+    def take_rows(e, x, cps):
         for cp in cps:
             cp.wait_recv()
         for s, r0 in ((0, 0), (1, rows + 2)):
             v = jnp.where(in_x[s], hr_rows[e, s].astype(F32), 0.0)
             for i in range(2):
                 x[(r0 + i) * width + 16:(r0 + i) * width + 16 + cols, :] = v[i * cols:(i + 1) * cols]
+
+    def take_rest(e, x, cps):
+        for cp in cps:
+            cp.wait_recv()
         for s, c0 in ((0, 14), (1, 16 + cols)):
             v = jnp.where(in_y[s], hr_cols[e, s].astype(F32), 0.0)
             for j in range(2):
@@ -175,6 +183,15 @@
                     [x[c + cols - 4:c + cols + 4, :], x[c - 4:c + 4, :]], axis=0)
                 s[r * 16:(r + 1) * 16, dj * chans:(dj + 1) * chans] = v.astype(BF16)
 
+    def side(x, r, dj):
+        c = (r + 2) * width + 15 + dj
+        return jnp.concatenate([x[c:c + 8, :], x[c + cols - 8:c + cols, :]], axis=0)
+
+    def widen_side(x, s):
+        for r in range(1, rows - 1):
+            for dj in range(3):
+                s[(r - 1) * 16:r * 16, dj * chans:(dj + 1) * chans] = side(x, r, dj).astype(BF16)
+
     def conv_pairs(a, w2x, first, pairs):
         v = jnp.concatenate([
             jnp.concatenate([a[(first + 2 * p + d) * cols:(first + 2 * p + d + 1) * cols, :]
@@ -187,7 +204,10 @@
         v = jnp.concatenate([s[d * 16:(d + rows + 2) * 16, :] for d in range(3)], axis=1)
         return jnp.dot(v, w[...], preferred_element_type=F32)
 
-    h_cot = rim_send(0, x_cot, cot_v)
+    ld_cot.wait()
+    fill(x_cot, cot_v)
+    h_cot = rim_rows(0, x_cot, cot_v)
+    h_cot2 = rim_cols(0, x_cot)
 
     third = 3 * chans
     ld_wb.wait()
@@ -219,9 +239,32 @@
     rest = ri % half
     perm = jnp.where(
         ci == (rest // span) * 2 * span + (ri // half) * span + rest % span, 1.0, 0.0).astype(BF16)
-    cot_t[...] = lax.dot_general(perm, cot_v[...], NT, preferred_element_type=F32).astype(BF16)
-
-    for cp in c1 + l1[2:4]:
+
+    def turn(v):
+        return lax.dot_general(perm, v, NT, preferred_element_type=F32)
+
+    lane = lax.broadcasted_iota(jnp.int32, (chans, (rows - 4) * cols), 1) % cols
+    inner = jnp.logical_and(lane >= 2, lane < cols - 2)
+    si = lax.broadcasted_iota(jnp.int32, (16, chans), 0)
+    outer = jnp.logical_or(si < 2, si >= 14)
+
+    def rows_and_sides(x):
+        v = [x[(r + 2) * width + 16:(r + 2) * width + 16 + cols, :]
+             for r in (0, 1, rows - 2, rows - 1)]
+        v += [jnp.where(outer, side(x, r, 1), 0.0) for r in range(2, rows - 2)]
+        return jnp.concatenate(v, axis=0).astype(BF16)
+
+    cot_t[...] = jnp.where(
+        inner, turn(cot_v[2 * cols:(rows - 2) * cols, :]), 0.0).astype(BF16)
+    cot_r[...] = turn(rows_and_sides(x_cot)).astype(BF16)
+    for x in (x_field, x_act):
+        for r in range(2, rows + 2):
+            x[r * width + 8:r * width + 16, :] = jnp.zeros((8, chans), F32)
+            x[r * width + 16 + cols:r * width + 24 + cols, :] = jnp.zeros((8, chans), F32)
+
+    for cp in ld_coarse:
+        cp.wait()
+    for cp in (l1[2], l1[3]):
         cp.wait_recv()
     ld_l = pltpu.make_async_copy(lrecv.at[pl.ds(2, 2)], lsm.at[pl.ds(2, 2)], lsem.at[0])
     ld_l.start()
@@ -230,18 +273,28 @@
     def clip(v):
         return jnp.minimum(jnp.maximum(v, 0), 2)
 
+    ids = [lists[0, k] for k in range(listed)]
+    wanted = [[lsm[i, k, 0] for k in range(listed)] for i in (2, 3)] + [ids]
+    spots = [[(clip(i // (nb * gy) - tx + 1), i % nb) for i in row] for row in wanted]
     c2 = []
-    for s in (2, 3):
-        for k in range(listed):
-            i = lsm[s, k, 0]
-            picked[s - 2, k] = call[clip(i // (nb * gy) - tx + 1), i % nb]
-        c2.append(remote(picked.at[s - 2], crecv.at[3 - s], csend.at[s], crcv.at[s], *around[s]))
-    ids = [lists[0, k] for k in range(listed)]
+    for h, cut in enumerate(cuts):
+        for cp in c1[h]:
+            cp.wait_recv()
+        for s in range(2):
+            for k in range(listed):
+                x, m = spots[s][k]
+                picked[s, h, k] = calls[h][x, m]
+            c2.append(remote(picked.at[s, h], crecv.at[1 - s, :, cut],
+                             c2s.at[h, s], c2r.at[h, s], *around[2 + s]))
     for k in range(listed):
-        i = ids[k]
-        crecv[2, k] = call[clip(i // (nb * gy) - tx + 1), i % nb]
-
-    rim_take(0, x_cot, h_cot)
+        x, m = spots[2][k]
+        for h in range(PARTS):
+            crecv[2, k, h * part:(h + 1) * part, :] = calls[h][x, m]
+
+    for i in (0, 1, 4, 5, 6, 7):
+        tell(i)
+    take_rows(0, x_cot, h_cot[:2])
+    take_rest(0, x_cot, h_cot[2:] + h_cot2)
     widen(x_cot, a_cot, 0, rows + 4, 0)
     widen_strip(x_cot, s_cot)
     for r, v in conv_pairs(a_cot, w2_bt, 0, (rows + 2) // 2):
@@ -256,13 +309,26 @@
         bt[k * cells:(k + 1) * cells, :] = crecv[which, k].astype(F32).T.astype(BF16)
     ld_fine.wait()
     ld_lift.wait()
-    g = jnp.dot(interp2[...], bt[...], preferred_element_type=F32).astype(BF16)
-    f = fine_v[...].astype(F32) + jnp.dot(g, lift_v[...], preferred_element_type=F32)
-    f = f.astype(BF16)
-    field[...] = f
-    fill(x_field, f)
-
-    h_field = rim_send(1, x_field, field)
+
+    def regrid(parts):
+        def cut(ref):
+            return jnp.concatenate([ref[p0 * cols:p1 * cols, :] for p0, p1 in parts], axis=0)
+        g = jnp.dot(cut(interp2), bt[...], preferred_element_type=F32).astype(BF16)
+        f = cut(fine_v).astype(F32) + jnp.dot(g, lift_v[...], preferred_element_type=F32)
+        f = f.astype(BF16)
+        o = 0
+        for p0, p1 in parts:
+            for r in range(p0, p1):
+                v = f[o:o + cols]
+                field[r * cols:(r + 1) * cols, :] = v
+                x_field[(r + 2) * width + 16:(r + 2) * width + 16 + cols, :] = v.astype(F32)
+                o += cols
+
+    regrid(((0, 2), (rows - 2, rows)))
+    h_rows = rim_rows(1, x_field, field)
+    regrid(((2, rows - 2),))
+
+    h_cols = rim_cols(1, x_field)
     widen(x_field, a_field, 2, rows + 2, 0)
 
     def point(pre, back):
@@ -277,15 +343,28 @@
 
     for r, pre in conv_pairs(a_field, w2_a, 2, (rows - 2) // 2):
         keep(r, pre)
-
-    rim_take(1, x_field, h_field)
+    widen(x_act, a_act, 3, rows + 1, 1)
+
+    def inner_grad(w, lhs, a, first):
+        v = jnp.concatenate(
+            [a[(first + d) * cols:(first + d + rows - 4) * cols, :] for d in range(3)], axis=1)
+        wsum[w] = jnp.dot(lhs, v, preferred_element_type=F32)
+
+    inner_grad(1, cot_t[...], a_act, 2)
+    bp_in = jnp.concatenate([x_bp[(r + 2) * width + 16:(r + 2) * width + 16 + cols, :]
+                             for r in range(2, rows - 2)], axis=0).astype(BF16)
+    inner_grad(0, jnp.where(inner, turn(bp_in), 0.0).astype(BF16), a_field, 3)
+
+    take_rows(1, x_field, h_rows[:2])
     widen(x_field, a_field, 0, 2, 0)
     widen(x_field, a_field, rows + 2, rows + 4, 0)
-    widen_edge(x_field, a_field, 2, rows + 2)
-    widen_strip(x_field, s_field)
     for r0 in (0, rows):
         for r, pre in conv_pairs(a_field, w2_a, r0, 1):
             keep(r, pre)
+    take_rest(1, x_field, h_cols + h_rows[2:])
+    widen_edge(x_field, a_field, 1, 5)
+    widen_edge(x_field, a_field, rows - 1, rows + 3)
+    widen_strip(x_field, s_field)
     pre = conv_strip(s_field, wa_v)
     act, bp = point(pre, ba_strip[...])
     inside = lax.broadcasted_iota(jnp.int32, (8, chans), 0)
@@ -303,10 +382,13 @@
             for x in (x_act, x_bp):
                 x[r * width:(r + 1) * width, :] = jnp.zeros((width, chans), F32)
 
-    def weight_grad(w, lhs, a, first):
-        v = jnp.concatenate([a[(first + d) * cols:(first + d) * cols + px, :] for d in range(3)],
-                            axis=1)
-        g = jnp.dot(lhs, v, preferred_element_type=F32)
+    def weight_grad(w, lhs, a, first, sides):
+        n = 2 * cols
+        v = jnp.concatenate([
+            jnp.concatenate([a[(first + d) * cols:(first + d) * cols + n, :],
+                             a[(first + d + rows - 2) * cols:(first + d + rows - 2) * cols + n, :],
+                             sides[d * 16:(d + rows - 4) * 16, :]], axis=0) for d in range(3)], axis=1)
+        g = wsum[w] + jnp.dot(lhs, v, preferred_element_type=F32)
         wsum[w] = g
         wsend[w] = g.astype(BF16)
 
@@ -354,21 +436,22 @@
             for u in range(3):
                 dst[3 * g + u] = acc[g * span:(g + 1) * span, u * chans:(u + 1) * chans]
 
-    widen(x_act, a_act, 1, rows + 3, 1)
-    weight_grad(1, cot_t[...], a_act, 0)
+    widen(x_act, a_act, 1, 5, 1)
+    widen(x_act, a_act, rows - 1, rows + 3, 1)
+    widen_side(x_act, side_act)
+    weight_grad(1, cot_r[...], a_act, 0, side_act)
     sb = first(1)
-    widen(x_bp, a_bp, 1, rows + 3, 1)
-    bp_t[...] = lax.dot_general(
-        perm, a_bp[cols:cols + px, chans:2 * chans], NT, preferred_element_type=F32).astype(BF16)
-    weight_grad(0, bp_t[...], a_field, 1)
+    widen_side(x_field, side_field)
+    weight_grad(0, turn(rows_and_sides(x_bp)).astype(BF16), a_field, 1, side_field)
     sa = first(0)
     sb = second(1, sb)
 
+    widen(x_bp, a_bp, 1, rows + 3, 1)
     bf = [(cot_v[r * cols:(r + 1) * cols, :].astype(F32) + v).astype(BF16)
           for r, v in conv_pairs(a_bp, w2_at, 0, rows // 2)]
+    sa = second(0, sa)
     br = lax.dot_general(lift_v[...], jnp.concatenate(bf, axis=0), NT,
                          preferred_element_type=F32).astype(BF16)
-    sa = second(0, sa)
     bb = jnp.dot(br, interp2[...], preferred_element_type=F32)
     for k in range(listed):
         v = bb[:, k * cells:(k + 1) * cells]
@@ -376,13 +459,11 @@
         gsend[k] = v.astype(BF16)
     d1 = [remote(gsend, g1.at[i ^ 1], gsnd.at[i], grcv.at[i], *around[i]) for i in range(8)]
 
+    widen(x_act, a_act, 3, rows + 1, 1)
     for r, v in conv_pairs(a_act, w2_b, 0, rows // 2):
         q = slice(r * cols, (r + 1) * cols)
-        out_v[q, :] = (field[q, :].astype(F32) + v).astype(BF16)
-    st_out = local(out_v, out, 7)
-
-    sb = last(1, sb)
-    sa = last(0, sa)
+        out[q, :] = (field[q, :].astype(F32) + v).astype(BF16)
+
     for i in (0, 1, 4, 5, 6, 7):
         l1[i].wait_recv()
     ld_m = [pltpu.make_async_copy(lrecv.at[pl.ds(i, n)], lsm.at[pl.ds(i, n)], lsem.at[j])
@@ -391,24 +472,32 @@
         cp.start()
     for cp in ld_m:
         cp.wait()
-    for cp in d1:
-        cp.wait_recv()
-    cand = [(ids[k], lambda k=k: gsum[k]) for k in range(listed)]
-    for s in range(8):
-        for k in range(listed):
-            cand.append((lsm[s, k, 0], lambda s=s, k=k: g1[s, k].astype(F32)))
     base = (tx * gy + ty) * nb
 
-    def total(m, _):
-        acc = jnp.zeros((chans_in, cells), F32)
-        for i, get in cand:
-            acc = acc + jnp.where(i == base + m, get(), 0.0)
-        gc[m] = acc
-        return 0
-    lax.fori_loop(0, nb, total, 0)
+    def add(start, cand):
+        def body(m, _):
+            acc = start(m)
+            for i, get in cand:
+                acc = acc + jnp.where(i == base + m, get(), 0.0)
+            gc[m] = acc
+            return 0
+        lax.fori_loop(0, nb, body, 0)
+
+    def arrive(group):
+        for s in group:
+            d1[s].wait_recv()
+        add(lambda m: gc[m], [(lsm[s, k, 0], lambda s=s, k=k: g1[s, k].astype(F32))
+                              for s in group for k in range(listed)])
+
+    add(lambda m: jnp.zeros((chans_in, cells), F32),
+        [(ids[k], lambda k=k: gsum[k]) for k in range(listed)])
+    sb = last(1, sb)
+    arrive((0, 1))
+    sa = last(0, sa)
+    arrive((2, 3))
+    arrive((4, 5, 6, 7))
     finish(1, sb, gb)
     finish(0, sa, ga)
-    st_out.wait()
     for cp in started:
         cp.wait_send()
 
@@ -434,20 +523,22 @@
     a_ext = vm(((rows + 4) * cols, 3 * chans), BF16)
     strip = vm(((rows + 4) * 16, 3 * chans), BF16)
     a_main = vm(((rows + 2) * cols, 3 * chans), BF16)
+    side = vm(((rows - 2) * 16, 3 * chans), BF16)
     w = vm((9 * chans, chans), BF16)
     w2 = vm((12 * chans, 2 * chans), BF16)
     scratch = [
-        vm((3, nb, ci, cells), BF16), vm((8, 128), jnp.int32), vm((8, 8, 128), jnp.int32),
-        pltpu.SMEM((8, 8, 128), jnp.int32), vm((2, listed, ci, cells), BF16),
+        vm((3, nb, ci // PARTS, cells), BF16), vm((3, nb, ci // PARTS, cells), BF16),
+        vm((8, 128), jnp.int32), vm((8, 8, 128), jnp.int32),
+        pltpu.SMEM((8, 8, 128), jnp.int32), vm((2, PARTS, listed, ci // PARTS, cells), BF16),
         vm((3, listed, ci, cells), BF16),
         vm((px * listed, cells), BF16), vm((px * listed // 8, cells), F32),
         vm((px, listed * cells), BF16), vm((px, chans), BF16), vm((ci, chans), BF16),
         w, w, w, w, w2, w2, w2, w2,
         vm((px, chans), BF16), vm((listed * cells, ci), BF16),
-        x, x, x, x, a_ext, a_ext, strip, strip, a_main, a_main,
+        x, x, x, x, a_ext, a_ext, strip, strip, a_main, a_main, side, side,
         vm(((rows + 2) * cols, chans), F32), vm(((rows + 2) * 16, chans), F32),
         vm((px, chans), BF16), vm((px, chans), BF16),
-        vm((chans, px), BF16), vm((chans, px), BF16),
+        vm((chans, (rows - 4) * cols), BF16), vm((chans, 4 * cols + (rows - 4) * 16), BF16),
         vm((2, 2, 2 * rows, chans), BF16), vm((2, 4, 16, chans), BF16),
         vm((2, 2, 2 * cols, chans), BF16), vm((2, 2, 2 * rows, chans), BF16),
         vm((2, 4, 16, chans), BF16),
@@ -458,7 +549,8 @@
         vm((2, sz.gy, sz.pack, 3 * chans), F32),
         vm((listed, ci, cells), F32), vm((listed, ci, cells), BF16),
         vm((8, listed, ci, cells), BF16),
-        dma((8,)), dma((3,)), dma((12,)), dma((12,)), dma((2, 8)), dma((2, 8)),
+        dma((8,)), dma((3,)), dma((12,)), dma((12,)),
+        dma((PARTS, 2)), dma((PARTS, 2)), dma((PARTS, 2)), dma((PARTS, 2)), dma((2, 8)), dma((2, 8)),
         dma((2, sz.plane + sz.gy)), dma((2, sz.plane + sz.gy)), dma((8,)), dma((8,)),
     ]
     flops = 2 * px * (6 * 9 * chans * chans + 2 * listed * cells * ci + 2 * ci * chans)
@@ -470,9 +562,9 @@
     )
     results = pl.pallas_call(
         functools.partial(kernel, sz),
-        out_shape=shapes,
+        out_shape=tuple(pltpu.VMEM(v.shape, v.dtype) for v in shapes),
         in_specs=[pl.BlockSpec(memory_space=pltpu.SMEM)] + [anyspace] * 7,
-        out_specs=(anyspace, vspace, vspace, vspace),
+        out_specs=(vspace, vspace, vspace, vspace),
         scratch_shapes=scratch,
         compiler_params=pltpu.CompilerParams(
             collective_id=0, has_side_effects=True, vmem_limit_bytes=56 * MIB),
@@ -484,6 +576,7 @@
         in_specs=[vspace] * 4,
         out_specs=(anyspace,) * 4,
         scratch_shapes=[dma((4,))],
+        compiler_params=pltpu.CompilerParams(vmem_limit_bytes=4 * MIB),
     )(*results)
 
 

time: 45.7 us -> 42.2 us (0.923); the launches traced: 45 us -> 42.1 us
  Pallas kernels: 44.3 us -> 41.3 us
    pallas_call x1, Pallas kernels: 42.3 us -> 40.4 us  [fused(): pl.pallas_call(functools.partial(kernel, sz), out_shape=tuple((pltpu.VMEM...]
    pallas_call x1, Pallas kernels: 2.06 us -> 0.93 us  [fused(): pl.pallas_call(hand_out, out_shape=shapes, in_specs=[vspace] * 4, out_spe...]
where the time goes in v3:
time: 42.2 us; the launch traced here: 42.1 us
  Pallas kernels  41.3 us (98%)
  between operations  0.8 us (2%)
    pallas_call x1, Pallas kernels, fused(): pl.pallas_call(functools.partial(kernel, sz), out_shape=tuple((pltpu.VMEM...  40.4 us
    pallas_call x1, Pallas kernels, fused(): pl.pallas_call(hand_out, out_shape=shapes, in_specs=[vspace] * 4, out_spe...  0.93 us

profile of v3, /device:TPU:0, one launch (start us, length us, event | category | flops | bytes accessed | tf_op | source)
XLA Modules:
  0.0 42.1 jit_solution(6887603082353625855)
XLA Ops:
  0.6 40.4 %shard_map.111 = (bf16[2048,128]{1,0:T(8,128)(2,1)S(1)}, f32[9,4,128]{2,1,0:T(4,128)S(1)}, f32[9,4,128]{2,1,0:T(4,128)S(1)}, f32[8,64,128]{2,1,0:T(8,128)S(1)}) custom-call(s32[1,4]{1,0:T(1,128)} %bitcast.21, bf16[8,64,128]{2,1,0:T(8,128)(2,1)} %bitcast.18, bf16[8192,128]{1,0:T(8,128)(2,1)} %bitcast.11, bf16[2048,128]{1,0:T(8,128)(2,1)} %bitcast.12, ...), custom_call_target="tpu_custom_call" | custom-call | flops 3959422976 | bytes 5242880 | tf_op jit(solution)/shard_map/pallas_call | solution.py:563
  41.0 0.9 %shard_map.112 = (bf16[2048,128]{1,0:T(8,128)(2,1)}, f32[9,4,128]{2,1,0:T(4,128)}, f32[9,4,128]{2,1,0:T(4,128)}, f32[8,64,128]{2,1,0:T(8,128)}) custom-call(bf16[2048,128]{1,0:T(8,128)(2,1)S(1)} %get-tuple-element.12.refs_0_, f32[9,4,128]{2,1,0:T(4,128)S(1)} %get-tuple-element.13.refs_1_, f32[9,4,128]{2,1,0:T(4,128)S(1)} %get-tuple-element.14.refs_2_, ...), custom_call_target="tpu_custom_call" | custom-call | tf_op jit(solution)/shard_map/pallas_call | solution.py:573

commit v4 on v3

--- a/solution.py
+++ b/solution.py
@@ -110,10 +110,7 @@
 
     def rim_rows(e, x, main):
         n2 = 2 * cols
-        cps = [remote(main.at[pl.ds(0, n2), :], hr_rows.at[e, 1],
-                      hsend.at[e, 0], hrcv.at[e, 0], *around[0]),
-               remote(main.at[pl.ds(px - n2, n2), :], hr_rows.at[e, 0],
-                      hsend.at[e, 1], hrcv.at[e, 1], *around[1])]
+        corners = []
         q = 0
         for r0, i0 in ((0, (4, 6)), (rows - 2, (7, 5))):
             for c0, i in ((0, i0[0]), (cols - 2, i0[1])):
@@ -121,10 +118,13 @@
                          for k in range(2)]
                 parts.append(jnp.zeros((12, chans), F32))
                 hs_corner[e, q] = jnp.concatenate(parts, axis=0).astype(BF16)
-                cps.append(remote(hs_corner.at[e, q], hr_corner.at[e, 3 - q],
-                                  hsend.at[e, 4 + q], hrcv.at[e, 4 + q], *around[i]))
+                corners.append(remote(hs_corner.at[e, q], hr_corner.at[e, 3 - q],
+                                      hsend.at[e, 4 + q], hrcv.at[e, 4 + q], *around[i]))
                 q += 1
-        return cps
+        return [remote(main.at[pl.ds(0, n2), :], hr_rows.at[e, 1],
+                       hsend.at[e, 0], hrcv.at[e, 0], *around[0]),
+                remote(main.at[pl.ds(px - n2, n2), :], hr_rows.at[e, 0],
+                       hsend.at[e, 1], hrcv.at[e, 1], *around[1])] + corners
 
     def rim_cols(e, x):
         for s, c0 in ((0, 0), (1, cols - 2)):
@@ -257,10 +257,17 @@
     cot_t[...] = jnp.where(
         inner, turn(cot_v[2 * cols:(rows - 2) * cols, :]), 0.0).astype(BF16)
     cot_r[...] = turn(rows_and_sides(x_cot)).astype(BF16)
-    for x in (x_field, x_act):
+    for x in (x_cot, x_field, x_act):
         for r in range(2, rows + 2):
             x[r * width + 8:r * width + 16, :] = jnp.zeros((8, chans), F32)
             x[r * width + 16 + cols:r * width + 24 + cols, :] = jnp.zeros((8, chans), F32)
+
+    def back(first, pairs):
+        for r, v in conv_pairs(a_cot, w2_bt, first, pairs):
+            ba_main[r * cols:(r + 1) * cols, :] = v
+
+    widen(x_cot, a_cot, 2, rows + 2, 0)
+    back(2, (rows - 2) // 2)
 
     for cp in ld_coarse:
         cp.wait()
@@ -294,11 +301,12 @@
     for i in (0, 1, 4, 5, 6, 7):
         tell(i)
     take_rows(0, x_cot, h_cot[:2])
+    widen(x_cot, a_cot, 0, 2, 0)
+    widen(x_cot, a_cot, rows + 2, rows + 4, 0)
+    back(0, 1)
+    back(rows, 1)
     take_rest(0, x_cot, h_cot[2:] + h_cot2)
-    widen(x_cot, a_cot, 0, rows + 4, 0)
     widen_strip(x_cot, s_cot)
-    for r, v in conv_pairs(a_cot, w2_bt, 0, (rows + 2) // 2):
-        ba_main[r * cols:(r + 1) * cols, :] = v
     ba_strip[...] = conv_strip(s_cot, wbt)
 
     for cp in c2:
@@ -332,7 +340,7 @@
     widen(x_field, a_field, 2, rows + 2, 0)
 
     def point(pre, back):
-        sig = 1.0 / (1.0 + jnp.exp(-pre))
+        sig = 0.5 + 0.5 * jnp.tanh(0.5 * pre)
         return pre * sig, back * (sig * (1.0 + pre * (1.0 - sig)))
 
     def keep(r, pre):
@@ -447,9 +455,13 @@
     sb = second(1, sb)
 
     widen(x_bp, a_bp, 1, rows + 3, 1)
-    bf = [(cot_v[r * cols:(r + 1) * cols, :].astype(F32) + v).astype(BF16)
-          for r, v in conv_pairs(a_bp, w2_at, 0, rows // 2)]
+    def back_rows(first):
+        return [(cot_v[r * cols:(r + 1) * cols, :].astype(F32) + v).astype(BF16)
+                for r, v in conv_pairs(a_bp, w2_at, first, rows // 4)]
+
+    bf = back_rows(0)
     sa = second(0, sa)
+    bf += back_rows(rows // 2)
     br = lax.dot_general(lift_v[...], jnp.concatenate(bf, axis=0), NT,
                          preferred_element_type=F32).astype(BF16)
     bb = jnp.dot(br, interp2[...], preferred_element_type=F32)

time: 42.2 us -> 42 us (level)
  no operation moved by 1% of the time
where the time goes in v4:
time: 42 us; the launch traced here: 41.9 us
  Pallas kernels  41.1 us (98%)
  between operations  0.8 us (2%)
    pallas_call x1, Pallas kernels, fused(): pl.pallas_call(functools.partial(kernel, sz), out_shape=tuple((pltpu.VMEM...  40.2 us
    pallas_call x1, Pallas kernels, fused(): pl.pallas_call(hand_out, out_shape=shapes, in_specs=[vspace] * 4, out_spe...  0.93 us

profile of v4, /device:TPU:0, one launch (start us, length us, event | category | flops | bytes accessed | tf_op | source)
XLA Modules:
  0.0 41.9 jit_solution(3102700885169024043)
XLA Ops:
  0.6 40.2 %shard_map.111 = (bf16[2048,128]{1,0:T(8,128)(2,1)S(1)}, f32[9,4,128]{2,1,0:T(4,128)S(1)}, f32[9,4,128]{2,1,0:T(4,128)S(1)}, f32[8,64,128]{2,1,0:T(8,128)S(1)}) custom-call(s32[1,4]{1,0:T(1,128)} %bitcast.21, bf16[8,64,128]{2,1,0:T(8,128)(2,1)} %bitcast.18, bf16[8192,128]{1,0:T(8,128)(2,1)} %bitcast.11, bf16[2048,128]{1,0:T(8,128)(2,1)} %bitcast.12, ...), custom_call_target="tpu_custom_call" | custom-call | flops 3959422976 | bytes 5242880 | tf_op jit(solution)/shard_map/pallas_call | solution.py:575
  40.8 0.9 %shard_map.112 = (bf16[2048,128]{1,0:T(8,128)(2,1)}, f32[9,4,128]{2,1,0:T(4,128)}, f32[9,4,128]{2,1,0:T(4,128)}, f32[8,64,128]{2,1,0:T(8,128)}) custom-call(bf16[2048,128]{1,0:T(8,128)(2,1)S(1)} %get-tuple-element.12.refs_0_, f32[9,4,128]{2,1,0:T(4,128)S(1)} %get-tuple-element.13.refs_1_, f32[9,4,128]{2,1,0:T(4,128)S(1)} %get-tuple-element.14.refs_2_, ...), custom_call_target="tpu_custom_call" | custom-call | tf_op jit(solution)/shard_map/pallas_call | solution.py:585
